TPU v7x, 128 devices: a whole 4x4x4 slice. The times are simulated.
128 devices in a mesh: leaf: 32 (over z, x, core), site: 4 (over y).
Axes of the slice: x: 4, y: 4, z: 4, core: 2. Of those that a mesh axis runs over, the one named last changes fastest.
Arguments:
- tip_states: int32 [4096, 512], P('leaf', 'site'), may hold values from 0 to 19
- local_len: float32 [32, 254], P('leaf'), may hold values from 0.02 to 0.5
- upper_len: float32 [32, 2], P('leaf'), may hold values from 0.02 to 0.5
- parent_lists: int32 [32, 254], P('leaf'), may hold values from 0 to 63, as said below
- exchange: float32 [20, 20], replicated, may hold values from 0.05 to 3, as said below
- freqs: float32 [20], replicated, may hold values from 0.02 to 0.1
- gamma_rates: float32 [4], replicated, may hold values from 0.1 to 2
Outputs:
- local_grad: float32 [32, 254], P('leaf')
- upper_grad: float32 [32, 2], P('leaf')
Inputs may be any that keep to these rules, and one draw needn't show every extreme that they name: `parent_lists`: in each group, the entries of one level of n nodes name every index 0 to n/2 - 1 exactly twice; levels stand in order, the 128 tips first. `exchange`: Symmetric; the diagonal does not enter.
All inputs are finite; a program needn't handle non-finite values.
Results may differ from a plain program's by a relative error of at most 0.0003.
Values sent between devices are 32-bit elements; how exact they have to be, the bound alone decides.
A program may use at most 320 MiB of HBM per device.

v0:
```python
import jax
import jax.numpy as jnp
from jax import lax
from jax.sharding import PartitionSpec as P

STATES = 20
RATES = 4
TERMS = 16
LEVELS = 7


highest = lax.Precision.HIGHEST


def from_behind(shard, axis, by):
    size = lax.axis_size(axis)
    pairs = [(i, i + by) for i in range(size) if 0 <= i + by < size]
    return lax.ppermute(shard, axis, pairs)


def model_tables(exchange, freqs):
    identity = jnp.eye(STATES, dtype=jnp.float32)
    root_prior = freqs / jnp.sum(freqs)
    off_rates = exchange * root_prior[None, :] * (1.0 - identity)
    outflow = jnp.sum(off_rates, axis=1)
    overall = jnp.sum(root_prior * outflow)
    rate_matrix = (off_rates - identity * outflow[:, None]) / overall
    uniform_rate = jnp.max(outflow / overall)
    step_matrix = identity + rate_matrix / uniform_rate
    powers = [identity]
    for power_no in range(TERMS):
        powers.append(jnp.dot(powers[-1], step_matrix, precision=highest))
    return (root_prior, uniform_rate, jnp.stack(powers).reshape(TERMS + 1, STATES * STATES))


def branch_tables(lengths, gamma_rates, uniform_rate, powers):
    number = lengths.shape[0]
    speeds = gamma_rates * uniform_rate
    scaled = lengths[:, None] * speeds[None, :]
    series = jnp.arange(TERMS + 1).astype(jnp.float32)
    log_factorial = jnp.cumsum(jnp.log(jnp.maximum(series, 1.0)))
    weights = jnp.exp(series * jnp.log(scaled)[:, :, None] - scaled[:, :, None] - log_factorial)
    shifted = jnp.concatenate([jnp.zeros_like(weights[:, :, :1]), weights[:, :, :-1]], axis=2)
    slopes = (shifted - weights) * speeds[None, :, None]
    combined = jnp.concatenate([weights, slopes], axis=1)
    matrices = jnp.einsum("nrk,km->nrm", combined, powers, precision=highest)
    matrices = matrices.reshape(number, 2 * RATES, STATES, STATES)
    return (matrices[:, :RATES], matrices[:, RATES:])


def apply_forward(matrices, vectors):
    return jnp.einsum("nrij,njrs->nirs", matrices, vectors, precision=highest)


def apply_back(matrices, vectors):
    return jnp.einsum("nrji,njrs->nirs", matrices, vectors, precision=highest)


def normalize(vectors):
    return vectors / jnp.max(vectors, axis=(1, 2), keepdims=True)


def upward(tip_block, lengths, parents, gamma_rates, uniform_rate, powers):
    tips_here = tip_block.shape[0]
    sites_here = tip_block.shape[1]
    state_ids = jnp.arange(STATES, dtype=jnp.int32)
    onehot = (tip_block[:, None, :] == state_ids[None, :, None]).astype(jnp.float32)
    partial_value = jnp.broadcast_to(onehot[:, :, None, :], (tips_here, STATES, RATES, sites_here))
    records = []
    offset = 0
    number = tips_here
    for height in range(LEVELS):
        forward, slopes = branch_tables(
            lengths[offset : offset + number], gamma_rates, uniform_rate, powers
        )
        message = apply_forward(forward, partial_value)
        sorted_ids = jnp.argsort(parents[offset : offset + number], stable=True)
        paired = message[sorted_ids].reshape(number // 2, 2, STATES, RATES, sites_here)
        records.append((partial_value, message, forward, slopes, sorted_ids))
        partial_value = normalize(paired[:, 0] * paired[:, 1])
        offset = offset + number
        number = number // 2
    return (partial_value, records)


def downward(from_above, records):
    pieces = []
    for height in reversed(range(LEVELS)):
        partial_value, message, forward, slopes, sorted_ids = records[height]
        number = partial_value.shape[0]
        paired = message[sorted_ids].reshape(number // 2, 2, STATES, RATES, partial_value.shape[3])
        sorted_pre = jnp.stack([from_above * paired[:, 1], from_above * paired[:, 0]], axis=1)
        inverse = jnp.argsort(sorted_ids, stable=True)
        outside = normalize(sorted_pre.reshape(partial_value.shape)[inverse])
        numerator = jnp.sum(outside * apply_forward(slopes, partial_value), axis=(1, 2))
        denominator = jnp.sum(outside * message, axis=(1, 2))
        pieces.insert(0, jnp.sum(numerator / denominator, axis=1))
        from_above = apply_back(forward, outside)
    return jnp.concatenate(pieces)


def per_device(tip_states, local_len, upper_len, parent_lists, exchange, freqs, gamma_rates):
    root_prior, uniform_rate, powers = model_tables(exchange, freqs)
    root_vec, records = upward(
        tip_states, local_len[0], parent_lists[0], gamma_rates, uniform_rate, powers
    )
    root_fwd, root_slope = branch_tables(upper_len[:, 0], gamma_rates, uniform_rate, powers)
    chain_fwd, chain_slope = branch_tables(upper_len[:, 1], gamma_rates, uniform_rate, powers)
    lifted = apply_forward(root_fwd, root_vec)
    all_ones = jnp.ones_like(lifted)
    prior_field = root_prior[None, :, None, None] * all_ones
    position = lax.axis_index("leaf")
    number = lax.axis_size("leaf")

    def lift_up(vector):
        return normalize(apply_forward(chain_fwd, lifted * vector))

    def lift_down(vector):
        return normalize(apply_back(chain_fwd, vector) * lifted)

    def forward_turn(step_no, carried):
        current, lower = carried
        incoming = from_behind(current, "leaf", 1)
        is_mine = position == step_no
        return (jnp.where(is_mine, lift_up(incoming), current), jnp.where(is_mine, incoming, lower))

    _, below = lax.fori_loop(1, number, forward_turn, (lift_up(all_ones), all_ones))

    def backward_turn(step_no, carried):
        sending, upper = carried
        incoming = from_behind(sending, "leaf", -1)
        is_mine = position == number - 1 - step_no
        return (
            jnp.where(is_mine, lift_down(incoming), sending),
            jnp.where(is_mine, incoming, upper),
        )

    _, outside = lax.fori_loop(1, number, backward_turn, (lift_down(prior_field), prior_field))
    beside_root = normalize(apply_back(chain_fwd, outside) * below)
    root_above = apply_back(root_fwd, beside_root)
    local_terms = downward(root_above, records)
    bottom = lifted * below
    chain_terms = jnp.sum(outside * apply_forward(chain_slope, bottom), axis=(1, 2)) / jnp.sum(
        outside * apply_forward(chain_fwd, bottom), axis=(1, 2)
    )
    root_terms = jnp.sum(beside_root * apply_forward(root_slope, root_vec), axis=(1, 2)) / jnp.sum(
        beside_root * lifted, axis=(1, 2)
    )
    upper_terms = jnp.stack([jnp.sum(root_terms[0]), jnp.sum(chain_terms[0])])
    local_total, upper_total = lax.psum((local_terms, upper_terms), "site")
    sites_total = tip_states.shape[1] * lax.axis_size("site")
    return ((local_total / sites_total)[None], (upper_total / sites_total)[None])


def solution(mesh):
    in_specs = (P("leaf", "site"), P("leaf", None), P("leaf", None), P("leaf", None), P(), P(), P())
    out_specs = (P("leaf", None), P("leaf", None))
    return jax.shard_map(
        per_device, mesh=mesh, in_specs=in_specs, out_specs=out_specs, check_vma=False
    )
```

profile of v0, /device:TPU:96, one launch (start us, length us, event | category | flops | bytes accessed | tf_op | source)
XLA Modules:
  0.0 767.0 jit_solution(1166887969927889386)
XLA Ops:
  21.0 6.8 copy.123
  28.0 14.4 %fusion.16 = f32[128,20,4,128]{3,1,2,0:T(8,128)} fusion(f32[128,4,20,20]{3,2,1,0:T(8,128)} %copy.123, f32[128,20,128]{2,1,0:T(8,128)S(1)} %fusion.24), kind=kOutput, calls=%fused_computation.48 | convolution fusion | flops 314572800 | bytes 7372800 | tf_op jit(solution)/shard_map/nrij,njrs->nirs/dot_general | solution.py:52
  44.9 6.4 gather_fusion
  61.3 10.1 %convolution_bitcast_fusion.1 = f32[64,20,4,128]{3,1,2,0:T(8,128)} fusion(f32[64,4,20,20]{2,3,1,0:T(8,128)S(1)} %copy.174, f32[64,128]{1,0:T(8,128)S(1)} %fusion.142, f32[64,2,20,4,128]{4,2,3,1,0:T(8,128)} %bitcast.629), kind=kOutput, calls=%fused_computation.49 | convolution fusion | flops 158597120 | bytes 8306688 | tf_op jit(solution)/shard_map/nrij,njrs->nirs/dot_general | solution.py:52
  133.7 240.1 %while.31 = (s32[]{:T(128)}, f32[1,20,4,128]{3,1,2,0:T(8,128)S(1)}, f32[1,20,4,128]{3,1,2,0:T(8,128)S(1)}, s32[]{:T(128)}, f32[1,4,20,20]{2,3,1,0:T(8,128)S(1)},...) while((s32[]{:T(128)}, f32[1,20,4,128]{3,1,2,0:T(8,128)S(1)}, f32[1,20,4,128]{3,1,2,0:T(8,128)S(1)}, ...), condition=%wide.region_22.23_spmd, body=%wide.region_20.22_spmd.sunk | while | flops 2508676 | bytes 540051 | solution.py:138
  139.6 5.8 collective-permute-start
  147.4 5.8 collective-permute-start
  163.0 5.8 collective-permute-start
  170.8 5.8 collective-permute-start
  178.7 5.8 collective-permute-start
  194.3 5.8 collective-permute-start
  202.1 5.8 collective-permute-start
  209.9 5.8 collective-permute-start
  217.7 5.8 collective-permute-start
  225.5 5.8 collective-permute-start
  241.1 5.8 collective-permute-start
  256.7 5.8 collective-permute-start
  272.3 5.8 collective-permute-start
  287.9 5.8 collective-permute-start
  303.6 5.8 collective-permute-start
  319.2 5.8 collective-permute-start
  334.8 5.8 collective-permute-start
  350.4 5.8 collective-permute-start
  366.0 5.8 collective-permute-start
  374.1 242.2 %while.32 = (s32[]{:T(128)}, f32[1,20,4,128]{3,1,2,0:T(8,128)S(1)}, f32[1,20,4,128]{3,1,2,0:T(8,128)S(1)}, s32[]{:T(128)}, f32[1,20,4,128]{3,1,2,0:T(8,128)S(1)}...) while((s32[]{:T(128)}, f32[1,20,4,128]{3,1,2,0:T(8,128)S(1)}, ...), condition=%wide.region_26.27_spmd.clone, body=%wide.region_24.26_spmd.clone.sunk | while | flops 2518916 | bytes 540057 | solution.py:127
  685.3 9.5 %fusion.8 = f32[64,128]{1,0:T(8,128)S(1)} fusion(f32[64,4,20,20]{3,2,1,0:T(8,128)} %copy.179, f32[64,128]{1,0:T(8,128)S(1)} %copy-done.20, f32[64,128]{1,0:T(8,128)S(1)} %reduce_max.200, f32[64,20,4,128]{3,2,1,0:T(4,128)S(1)} %gather_fusion.12, f32[64,2,20,4,128]{4,2,3,1,0:T(8,128)} %bitcast.630), kind=kOutput, calls=%fused_computation.36 | convolution fusion | flops 160555008 | bytes 8372224 | tf_op jit(solution)/shard_map/nrij,njrs->nirs/dot_general | solution.py:52
  694.9 7.7 %fusion.9 = (f32[64,1,20,4,128]{4,2,3,0,1:T(8,128)S(1)}, f32[64,1,20,4,128]{4,2,3,0,1:T(8,128)S(1)}) fusion(f32[64,2,20,4,128]{4,2,3,1,0:T(8,128)} %bitcast.631, f32[64,4,20,20]{2,3,1,0:T(8,128)S(1)} %copy-done.3, f32[64,20,4,128]{3,2,1,0:T(4,128)S(1)} %gather_fusion.12, f32[64,128]{1,0:T(8,128)S(1)} %reduce_max.200), kind=kOutput, calls=%fused_computation.39 | convolution fusion | flops 159252480 | bytes 13549568 | tf_op jit(solution)/shard_map/nrji,njrs->nirs/dot_general | solution.py:56
  715.4 8.2 %gather_fusion.13 = f32[128,20,4,128]{3,2,1,0:T(4,128)} fusion(f32[128,20,4,128]{3,2,1,0:T(4,128)} %copy.176, s32[1024]{0:T(1024)S(1)} %pad_clamp_fusion), kind=kCustom, calls=%fused_computation.13 | custom fusion | bytes 10486272 | tf_op jit(solution)/shard_map/gather | solution.py:94
  728.7 6.4 multiply_reduce_fusion
  735.1 6.3 copy.178
  741.4 13.4 %fusion.7 = f32[128,128]{1,0:T(8,128)S(1)} fusion(f32[128,128]{1,0:T(8,128)S(1)} %reduce_max.201, f32[128,20,4,128]{3,2,1,0:T(4,128)} %gather_fusion.13, f32[128,4,20,20]{3,2,1,0:T(8,128)} %copy.178, f32[128,20,128]{2,1,0:T(8,128)S(1)} %copy-done.5), kind=kOutput, calls=%fused_computation.29 | convolution fusion | flops 318488576 | bytes 7503872 | tf_op jit(solution)/shard_map/nrij,njrs->nirs/dot_general | solution.py:52
  755.0 10.7 %all-reduce.9 = (f32[254]{0:T(256)S(1)}, f32[2]{0:T(128)S(1)}) all-reduce(f32[254]{0:T(256)S(1)} %concatenate.76, f32[2]{0:T(128)S(1)} %pad_maximum_fusion.6), channel_id=1, replica_groups=mesh['leaf'=32,'site'=4] {'site'}, use_global_device_ids=true, to_apply=%region_63.64 | all-reduce | flops 256 | bytes 2048 | tf_op jit(solution)/shard_map/psum | solution.py:150
  (584 shorter events, 551.5 us)
Async XLA Ops:
  139.6 7.5 collective-permute-start
  147.4 7.5 collective-permute-start
  155.2 7.5 collective-permute-start
  163.0 7.5 collective-permute-start
  170.8 7.5 collective-permute-start
  178.7 7.5 collective-permute-start
  186.5 7.5 collective-permute-start
  194.3 7.5 collective-permute-start
  202.1 7.5 collective-permute-start
  209.9 7.5 collective-permute-start
  217.7 7.5 collective-permute-start
  225.5 7.5 collective-permute-start
  233.3 7.5 collective-permute-start
  241.1 7.5 collective-permute-start
  248.9 7.5 collective-permute-start
  256.7 7.5 collective-permute-start
  264.5 7.5 collective-permute-start
  272.3 7.5 collective-permute-start
  280.1 7.5 collective-permute-start
  287.9 7.5 collective-permute-start
  295.7 7.5 collective-permute-start
  303.6 7.5 collective-permute-start
  311.4 7.5 collective-permute-start
  319.2 7.5 collective-permute-start
  327.0 7.5 collective-permute-start
  334.8 7.5 collective-permute-start
  342.6 7.5 collective-permute-start
  350.4 7.5 collective-permute-start
  358.2 7.5 collective-permute-start
  366.0 7.5 collective-permute-start
  374.1 7.6 collective-permute-start.1
  491.3 7.5 collective-permute-start.1
  (74 other events, 1238.1 us)
where the time goes:
time: 773 us; the launch traced here: 767 us
  starting transfers between devices  237 us (31%)
  waiting for transfers between devices  226 us (29%)
  matrix products  123 us (16%)
  local copies, waits for them, and re-layouts  101 us (13%)
  other arithmetic  63.1 us (8%)
  blocking collectives  10.7 us (1%)
    ppermute x62, starting transfers between devices, from_behind(): return lax.ppermute(shard, axis, pairs)  237 us
    ppermute x62, waiting for transfers between devices, from_behind(): return lax.ppermute(shard, axis, pairs)  226 us
    dot_general x50, matrix products, apply_forward(): return jnp.einsum('nrij,njrs->nirs', matrices, vectors, precision=highest)  82.4 us
    slice x17, local copies, waits for them, and re-layouts, branch_tables(): return (matrices[:, :RATES], matrices[:, RATES:])  36.8 us
    dot_general x40, matrix products, apply_back(): return jnp.einsum('nrji,njrs->nirs', matrices, vectors, precision=highest)  25.1 us
    gather x7, local copies, waits for them, and re-layouts, downward(): outside = normalize(sorted_pre.reshape(partial_value.shape)[inverse])  18.7 us
    gather x7, local copies, waits for them, and re-layouts, upward(): message[sorted_ids].reshape(number // 2, 2, STATES, RATES, sites_here)  17.1 us
  transfers between devices with their start and end apart: 62, of which 62 were waited for; matrix products, arithmetic and copies ran while one was open for 0% of the time, Pallas kernels for 0%

commit v1 on v0

v1 whole, which is shorter than its diff:
```python
import math

import jax
import jax.numpy as jnp
from jax import lax
from jax.experimental import pallas as pl
from jax.experimental.pallas import tpu as pltpu
from jax.sharding import PartitionSpec as P

STATES = 20
RATES = 4
TERMS = 16
TIPS = 128
BLOCK = STATES * RATES
LANES = 128
MESH = pl.DeviceIdType.MESH
LEVEL_BASE = (0, 64, 96, 112, 120, 124, 126)

f32 = jnp.float32
bf16 = jnp.bfloat16
i32 = jnp.int32


def iota(shape, dim):
    return lax.broadcasted_iota(i32, shape, dim)


def lookup(table, index):
    return jnp.take_along_axis(table, index, axis=1, mode="promise_in_bounds")


def dot(a, b):
    return jnp.dot(a, b, preferred_element_type=f32)


def halves(x):
    high = x.astype(bf16)
    return high, (x - high.astype(f32)).astype(bf16)


def staircase(lane, starts, values):
    out = jnp.full(lane.shape, values[0], i32)
    for start, value in zip(starts[1:], values[1:]):
        out = jnp.where(lane >= start, value, out)
    return out


def pack_matrix(table):
    lane = iota((8, LANES), 1)[:1]
    high = table.astype(bf16).astype(f32)
    low = table - high
    inner = lane < BLOCK
    first = jnp.concatenate([high[:40], jnp.where(inner, high[40:], 0.0)], axis=0)
    second = jnp.concatenate([jnp.where(inner, low[:40], 0.0), jnp.where(inner, low[40:], high[40:])], axis=0)
    return jnp.concatenate([first.astype(bf16), second.astype(bf16)], axis=1)


def pack_vector(x):
    high = x.astype(bf16)
    low = x - high.astype(f32)
    gap = jnp.zeros((8, LANES), f32)
    low_first = jnp.concatenate([low[:40], gap], axis=0).astype(bf16)
    low_second = jnp.concatenate([low[40:], gap], axis=0).astype(bf16)
    return jnp.concatenate([high, low_first, high, low_second], axis=0)


def kernel(
    tips_ref, lens_ref, parents_ref, exchange_ref, freqs_ref, gamma_ref, out_ref,
    pad, powers, pi_rows, pi_block, tip_rhs, node_rhs, tip_table, node_table, packed,
    tip_pos, partial1, partial, message, slope, above, norm, acc, acc_tip, place,
    chain_table, chain_rhs, len_src, len_all, lift_t, lift_all, z_out, z_in, sum_src, sum_all,
    len_send, len_recv, lift_send, lift_recv, z_send, z_recv, sum_send, sum_recv,
):
    me = lax.axis_index("leaf")
    site = lax.axis_index("site")
    groups = lax.axis_size("leaf")
    site_devs = lax.axis_size("site")

    def leaf_peer(offset):
        return lax.rem(me + offset, groups)

    barrier = pltpu.get_barrier_semaphore()

    def greet_leaf(offset, carry):
        pl.semaphore_signal(barrier, inc=1, device_id=(leaf_peer(offset), site), device_id_type=MESH)
        return carry

    def greet_site(offset, carry):
        pl.semaphore_signal(
            barrier, inc=1, device_id=(me, lax.rem(site + offset, site_devs)), device_id_type=MESH
        )
        return carry

    lax.fori_loop(1, groups, greet_leaf, 0)
    lax.fori_loop(1, site_devs, greet_site, 0)

    lane = iota((8, LANES), 1)[:1]
    square_lane = iota((LANES, LANES), 1)
    square_row = iota((LANES, LANES), 0)

    tip_parent = parents_ref[0:1, :]
    raw_parent = parents_ref[1:2, :]
    own_base = staircase(lane, LEVEL_BASE, LEVEL_BASE)
    next_base = staircase(lane, LEVEL_BASE, LEVEL_BASE[1:] + (126,))
    half = staircase(lane, LEVEL_BASE, (32, 16, 8, 4, 2, 1, 0))
    is_node = lane < 126
    node_parent = jnp.where(is_node, raw_parent + next_base, lane)

    def second_child(parent_row):
        across = jnp.broadcast_to(parent_row.astype(f32), (LANES, LANES))
        down = jnp.transpose(across)
        hit = (across == down) & (square_row < square_lane)
        return jnp.max(jnp.where(hit, 1.0, 0.0), axis=0, keepdims=True).astype(i32)

    node_second = second_child(jnp.where(is_node, node_parent, lane + 200))
    tip_second = second_child(tip_parent)
    position = lane
    for _ in range(6):
        found = lookup(jnp.broadcast_to(position, (8, LANES)), jnp.broadcast_to(node_parent, (8, LANES)))[:1]
        position = jnp.where(is_node, own_base + node_second * half + found - next_base, lane)
    found = lookup(jnp.broadcast_to(position, (8, LANES)), jnp.broadcast_to(tip_parent, (8, LANES)))[:1]
    tip_position = tip_second * 64 + found
    tip_place = jnp.where(square_row == tip_position, 1.0, 0.0)
    node_place = jnp.where(square_row == position, 1.0, 0.0)
    place[0] = tip_place
    place[1] = node_place
    tip_pos[...] = dot(tip_place.astype(bf16), tips_ref[...].astype(f32).astype(bf16)).astype(i32)
    tip_len = jnp.sum(tip_place * lens_ref[0:1, :], axis=1, keepdims=True)
    node_len = jnp.sum(node_place * lens_ref[1:2, :], axis=1, keepdims=True)

    pad[...] = jnp.zeros_like(pad)
    pad[0:20, 0:20] = exchange_ref[...]
    pad[24:25, 0:20] = freqs_ref[...]
    freqs = pad[24:25, :]
    pi_row = freqs / jnp.sum(freqs, axis=1, keepdims=True)
    row24 = iota((24, LANES), 0)
    lane24 = iota((24, LANES), 1)
    eye = jnp.where((row24 == lane24) & (row24 < STATES), 1.0, 0.0)
    off = pad[0:24, :] * pi_row * (1.0 - eye)
    outflow = jnp.sum(off, axis=1, keepdims=True)
    pi_col = jnp.sum(eye * pi_row, axis=1, keepdims=True)
    overall = jnp.sum(pi_col * outflow, axis=0, keepdims=True)
    fastest = jnp.max(outflow, axis=0, keepdims=True)
    uniform = fastest / overall
    step = eye + (off - eye * outflow) / fastest

    def repeat(x):
        twice = x + pltpu.roll(x, 20, 1)
        return twice + pltpu.roll(twice, 40, 1) + pltpu.roll(twice, 80, 1)

    rest = jnp.zeros((104, LANES), f32)

    def advance(rows, by):
        return jnp.dot(
            rows, jnp.concatenate([by, rest], axis=0), precision=lax.Precision.HIGHEST, preferred_element_type=f32
        )

    powers[...] = jnp.zeros_like(powers)
    powers[0:24, :] = repeat(eye)
    first = repeat(step)
    powers[24:48, :] = first
    second = advance(first, first)
    powers[48:72, :] = second
    upto4 = advance(powers[24:72, :], second)
    powers[72:120, :] = upto4
    upto8 = advance(powers[24:120, :], upto4[24:48])
    powers[120:216, :] = upto8
    powers[216:408, :] = advance(powers[24:216, :], upto8[72:96])

    pi_bcast = jnp.broadcast_to(pi_col, (24, LANES))
    pi_rows[...] = pi_bcast
    for c in range(RATES):
        pi_block[20 * c : 20 * c + 20, :] = pi_bcast[0:20, :]

    lane_block = staircase(lane, (0, 20, 40, 60, 80, 100, 120), (0, 1, 2, 3, 4, 5, 6))
    term = lane & 31
    term_f = term.astype(f32)
    log_factorial = jnp.zeros((1, LANES), f32)
    for m in range(2, TERMS + 1):
        log_factorial = log_factorial + jnp.where(term >= m, math.log(m), 0.0)

    def weights(lengths, c, with_slope):
        speed = gamma_ref[c] * uniform
        tau = lengths * speed
        w = jnp.exp(term_f * jnp.log(tau) - tau - log_factorial)
        w = jnp.where(term <= TERMS, w, 0.0)

        def lay(value):
            high = value.astype(bf16).astype(f32)
            return jnp.where(lane < 64, high, value - high).astype(bf16)

        if not with_slope:
            return lay(w)
        return jnp.concatenate([lay(w), lay(w * (term_f / lengths - speed))], axis=0)

    def stack_terms(x):
        high, low = halves(x)
        return jnp.concatenate([high, low, high, low], axis=0)

    pi_tiles = []
    tiles = []
    for a in range(4):
        tile = jnp.zeros((32, LANES), f32)
        pi_tile = jnp.zeros((1, LANES), f32)
        for b in range(6):
            i = 6 * a + b
            if i < STATES:
                tile = jnp.where(lane_block == b, powers[pl.ds(i, 32, stride=24), :], tile)
                pi_tile = jnp.where(lane_block == b, pi_rows[i : i + 1, :], pi_tile)
        tiles.append(stack_terms(tile))
        pi_tiles.append(pi_tile)
    for a in range(4):
        tip_rhs[:, LANES * a : LANES * (a + 1)] = tiles[a]
    tip_lengths = jnp.broadcast_to(tip_len, (TIPS, LANES))
    node_lengths = jnp.broadcast_to(node_len, (TIPS, LANES))
    node_weights = []
    for c in range(RATES):
        w_tip = weights(tip_lengths, c, True)
        for a in range(4):
            made = dot(w_tip, tip_rhs[:, LANES * a : LANES * (a + 1)])
            tip_table[c, 0:128, LANES * a : LANES * (a + 1)] = made[:128]
            tip_table[c, 128:256, LANES * a : LANES * (a + 1)] = made[128:] * pi_tiles[a]
        node_weights.append(weights(node_lengths, c, True))

    pl.semaphore_wait(barrier, groups - 1 + site_devs - 1)
    chain_len = jnp.broadcast_to(node_len[127:128, :], (8, LANES))
    len_src[...] = chain_len
    len_all[me] = chain_len

    def len_copy(offset, slot):
        return pltpu.make_async_remote_copy(
            src_ref=len_src, dst_ref=len_all.at[slot], send_sem=len_send.at[offset], recv_sem=len_recv.at[slot],
            device_id=(leaf_peer(offset), site), device_id_type=MESH,
        )

    def start_len(offset, carry):
        len_copy(offset, me).start()
        return carry

    lax.fori_loop(1, groups, start_len, 0)

    keeps = []
    for c in range(RATES):
        keep = (lane_block == c) | (lane_block == 4 + c % 2)
        keeps.append(jnp.where(keep, 1.0, 0.0).astype(bf16))

    def node_row(i, carry):
        stacked = stack_terms(powers[pl.ds(i, 32, stride=24), :])
        scale = pi_rows[pl.ds(i, 1), :]
        for c in range(RATES):
            rhs = stacked * keeps[c]
            node_rhs[c * STATES + i] = rhs
            made = dot(node_weights[c], rhs)
            node_table[0, pl.ds((c * STATES + i) * TIPS, TIPS), :] = made[:128]
            node_table[1, pl.ds((c * STATES + i) * TIPS, TIPS), :] = made[128:] * scale
        return carry

    lax.fori_loop(0, STATES, node_row, 0)

    def tips_up(o, carry):
        left = pl.multiple_of(8 * o, 8)
        left_state = tip_pos[pl.ds(left, 8), :]
        right_state = tip_pos[pl.ds(left + 64, 8), :]
        for b in range(6):
            left_index = left_state + 20 * b
            right_index = right_state + 20 * b
            for c in range(RATES):
                for a in range(4):
                    i = 6 * a + b
                    if i < STATES:
                        at = pl.ds(LANES * a, LANES)
                        x = lookup(tip_table[c, pl.ds(left, 8), at], left_index)
                        y = lookup(tip_table[c, pl.ds(left + 64, 8), at], right_index)
                        partial1[pl.ds(64 * (c * STATES + i) + left, 8), :] = x * y
        return carry

    lax.fori_loop(0, 8, tips_up, 0)

    def node_up(node, x):
        matrix = pack_matrix(node_table[0, pl.ds(node, BLOCK, stride=TIPS), :])
        derivative = pack_matrix(node_table[1, pl.ds(node, BLOCK, stride=TIPS), :])
        packed[node] = matrix
        made = dot(jnp.concatenate([matrix, derivative], axis=0), pack_vector(x))
        message[node] = made[:BLOCK]
        slope[node] = made[BLOCK:]
        return made[:BLOCK]

    def read_partial(level, node):
        if level == 1:
            return partial1[pl.ds(node, BLOCK, stride=64), :]
        return partial[node]

    for level in range(1, 7):
        base, after = LEVEL_BASE[level - 1], LEVEL_BASE[level]
        pairs = 64 >> level
        batch = min(pairs, 4)

        def pairs_up(turn, carry):
            for part in range(batch):
                m = turn * batch + part
                x = node_up(base + m, read_partial(level, base + m))
                y = node_up(base + pairs + m, read_partial(level, base + pairs + m))
                product = x * y
                factor = 1.0 / jnp.max(product, axis=0, keepdims=True)
                norm[after + m] = jnp.broadcast_to(factor, (8, LANES))
                partial[after + m] = product * factor
            return carry

        lax.fori_loop(0, pairs // batch, pairs_up, 0)

    lifted = node_up(126, partial[126])

    lift_t[...] = jnp.transpose(jnp.concatenate([lifted, jnp.zeros((LANES - BLOCK, LANES), f32)], axis=0))
    pair_no = me // 2
    side = lax.rem(me, 2)
    lift_all[me] = lift_t[pl.ds(pl.multiple_of(8 * pair_no, 8), 8), :]

    def lift_copy(offset, slot):
        peer = leaf_peer(offset)
        return pltpu.make_async_remote_copy(
            src_ref=lift_t.at[pl.ds(pl.multiple_of(8 * (peer // 2), 8), 8), :], dst_ref=lift_all.at[slot],
            send_sem=lift_send.at[offset], recv_sem=lift_recv.at[slot],
            device_id=(peer, site), device_id_type=MESH,
        )

    def start_lift(offset, carry):
        lift_copy(offset, me).start()
        return carry

    lax.fori_loop(1, groups, start_lift, 0)

    def wait_len(offset, carry):
        len_copy(offset, leaf_peer(offset)).wait_recv()
        len_copy(offset, me).wait_send()
        return carry

    lax.fori_loop(1, groups, wait_len, 0)
    chain_lengths = len_all[:, 0, :]
    chain_weights = [weights(chain_lengths, c, False) for c in range(RATES)]

    def chain_row(i, carry):
        for c in range(RATES):
            made = dot(chain_weights[c], node_rhs[c * STATES + i])
            chain_table[pl.ds((c * STATES + i) * 32, 32), :] = made
        return carry

    lax.fori_loop(0, STATES, chain_row, 0)

    def chain_pack(g, carry):
        matrix = jnp.where(lane < BLOCK, chain_table[pl.ds(g, BLOCK, stride=32), :], 0.0)
        high, low = halves(matrix)
        chain_rhs[g, 0:BLOCK, 0:LANES] = high
        chain_rhs[g, 0:BLOCK, LANES:] = low
        return carry

    lax.fori_loop(0, groups, chain_pack, 0)

    def wait_lift(offset, carry):
        lift_copy(offset, leaf_peer(offset)).wait_recv()
        lift_copy(offset, me).wait_send()
        return carry

    lax.fori_loop(1, groups, wait_lift, 0)

    def z_copy(source, group, to_side, row, slot):
        return pltpu.make_async_remote_copy(
            src_ref=z_out.at[source], dst_ref=z_in.at[to_side, pl.ds(pl.multiple_of(8 * row, 8), 8), :],
            send_sem=z_send.at[source], recv_sem=z_recv.at[slot],
            device_id=(group, site), device_id_type=MESH,
        )

    pi_lanes = jnp.where(lane < BLOCK, repeat(jnp.broadcast_to(pi_row, (8, LANES)))[:1], 0.0)
    is_up = side == 0

    def chain_step(t, z):
        g = jnp.where(is_up, t, groups - 1 - t)
        z_out[g] = z

        @pl.when(g != me)
        def _():
            z_copy(g, g, side, pair_no, me).start()

        lift = lift_all[g]
        before = jnp.where(is_up, lift, 1.0) * z
        factor = jnp.where(is_up, 1.0, lift) / jnp.max(before, axis=1, keepdims=True)
        high, low = halves(before)
        made = dot(jnp.concatenate([high, low], axis=0)[:, :BLOCK], chain_rhs[g])
        return (made[0:8, :LANES] + (made[8:16, :LANES] + made[0:8, LANES:])) * factor

    z = lax.fori_loop(0, groups, chain_step, jnp.broadcast_to(pi_lanes, (8, LANES)))
    z_in[side, pl.ds(pl.multiple_of(8 * pair_no, 8), 8), :] = z_out[me]

    def wait_z(offset, carry):
        peer = leaf_peer(offset)
        z_copy(peer, peer, lax.rem(peer, 2), peer // 2, peer).wait_recv()
        z_copy(peer, peer, side, pair_no, me).wait_send()
        return carry

    lax.fori_loop(1, groups, wait_z, 0)

    pi80 = pi_block[...]
    below = jnp.transpose(z_in[0])[:BLOCK] / pi80
    outside = jnp.transpose(z_in[1])[:BLOCK] / pi80
    chain_matrix = pack_matrix(node_table[0, pl.ds(127, BLOCK, stride=TIPS), :])
    chain_derivative = pack_matrix(node_table[1, pl.ds(127, BLOCK, stride=TIPS), :])
    lifted = message[126]
    beside = dot(chain_matrix, pack_vector(outside)) * below
    scale = 1.0 / jnp.max(beside, axis=0, keepdims=True)
    beside = beside * scale
    outside = outside * scale
    scale = 1.0 / jnp.sum(pi80 * beside * lifted, axis=0, keepdims=True)
    beside = beside * scale
    outside = outside * scale
    chain_slope = dot(chain_derivative, pack_vector(lifted * below))

    def fold(x):
        total = x[0:8]
        for k in range(1, BLOCK // 8):
            total = total + x[8 * k : 8 * k + 8]
        return total

    acc[pl.ds(8 * 127, 8), :] = fold(outside * chain_slope)
    acc[pl.ds(8 * 126, 8), :] = fold(beside * slope[126])
    above[pl.ds(BLOCK * 126, BLOCK), :] = dot(packed[126], pack_vector(beside))

    def node_down(node, pre):
        acc[pl.ds(pl.multiple_of(8 * node, 8), 8), :] = fold(pre * slope[node])
        made = dot(packed[node], pack_vector(pre))
        above[pl.ds(pl.multiple_of(BLOCK * node, 8), BLOCK), :] = made

    for level in range(6, 0, -1):
        base, after = LEVEL_BASE[level - 1], LEVEL_BASE[level]
        pairs = 64 >> level
        batch = min(pairs, 4)

        def pairs_down(turn, carry):
            for part in range(batch):
                m = turn * batch + part
                parent = after + m
                left, right = base + m, base + pairs + m
                over = above[pl.ds(pl.multiple_of(BLOCK * parent, 8), BLOCK), :] * norm[parent][:1]
                node_down(left, over * message[right])
                node_down(right, over * message[left])
            return carry

        lax.fori_loop(0, pairs // batch, pairs_down, 0)

    def tips_down(o, carry):
        left = pl.multiple_of(8 * o, 8)
        left_state = tip_pos[pl.ds(left, 8), :]
        right_state = tip_pos[pl.ds(left + 64, 8), :]
        left_sum = jnp.zeros((8, LANES), f32)
        right_sum = jnp.zeros((8, LANES), f32)
        for b in range(6):
            left_index = left_state + 20 * b
            right_index = right_state + 20 * b
            for c in range(RATES):
                for a in range(4):
                    i = 6 * a + b
                    if i < STATES:
                        at = pl.ds(LANES * a, LANES)
                        over = above[pl.ds(BLOCK * left + c * STATES + i, 8, stride=BLOCK), :]
                        left_message = lookup(tip_table[c, pl.ds(left, 8), at], left_index)
                        right_message = lookup(tip_table[c, pl.ds(left + 64, 8), at], right_index)
                        left_slope = lookup(tip_table[c, pl.ds(left + 128, 8), at], left_index)
                        right_slope = lookup(tip_table[c, pl.ds(left + 192, 8), at], right_index)
                        left_sum = left_sum + over * right_message * left_slope
                        right_sum = right_sum + over * left_message * right_slope
        acc_tip[pl.ds(left, 8), :] = left_sum
        acc_tip[pl.ds(left + 64, 8), :] = right_sum
        return carry

    lax.fori_loop(0, 8, tips_down, 0)

    tip_total = jnp.sum(acc_tip[...], axis=1, keepdims=True)
    folded = acc[pl.ds(0, TIPS, stride=8), :]
    for k in range(1, 8):
        folded = folded + acc[pl.ds(k, TIPS, stride=8), :]
    node_total = jnp.sum(folded, axis=1, keepdims=True)
    tip_row = jnp.sum(place[0] * tip_total, axis=0, keepdims=True)
    node_row_ = jnp.sum(place[1] * node_total, axis=0, keepdims=True)
    share = jnp.concatenate([tip_row, node_row_, jnp.zeros((6, LANES), f32)], axis=0)
    share = share * (1.0 / (LANES * site_devs))
    sum_src[...] = share
    sum_all[site] = share

    def sum_copy(offset, slot):
        return pltpu.make_async_remote_copy(
            src_ref=sum_src, dst_ref=sum_all.at[slot], send_sem=sum_send.at[offset], recv_sem=sum_recv.at[slot],
            device_id=(me, lax.rem(site + offset, site_devs)), device_id_type=MESH,
        )

    for offset in range(1, site_devs):
        sum_copy(offset, site).start()
    for offset in range(1, site_devs):
        sum_copy(offset, lax.rem(site + offset, site_devs)).wait_recv()
        sum_copy(offset, site).wait_send()
    total = sum_all[0]
    for k in range(1, site_devs):
        total = total + sum_all[k]
    out_ref[...] = total


def per_device(tip_states, local_len, upper_len, parent_lists, exchange, freqs, gamma_rates):
    groups = lax.axis_size("leaf")
    site_devs = lax.axis_size("site")
    lens = jnp.concatenate([local_len, upper_len], axis=1).reshape(2, LANES)
    parents = jnp.concatenate([parent_lists, jnp.zeros((1, 2), i32)], axis=1).reshape(2, LANES)
    vmem = pl.BlockSpec(memory_space=pltpu.VMEM)
    smem = pl.BlockSpec(memory_space=pltpu.SMEM)
    V = pltpu.VMEM
    D = pltpu.SemaphoreType.DMA
    total = pl.pallas_call(
        kernel,
        out_shape=jax.ShapeDtypeStruct((8, LANES), f32),
        in_specs=[vmem] * 5 + [smem],
        out_specs=vmem,
        scratch_shapes=[
            V((32, LANES), f32),
            V((32 * 24, LANES), f32),
            V((24, LANES), f32),
            V((BLOCK, LANES), f32),
            V((LANES, 4 * LANES), bf16),
            V((BLOCK, LANES, LANES), bf16),
            V((RATES, 2 * TIPS, 4 * LANES), f32),
            V((2, BLOCK * TIPS, LANES), f32),
            V((TIPS, BLOCK, 2 * LANES), bf16),
            V((TIPS, LANES), i32),
            V((BLOCK * 64, LANES), f32),
            V((TIPS, BLOCK, LANES), f32),
            V((TIPS, BLOCK, LANES), f32),
            V((TIPS, BLOCK, LANES), f32),
            V((TIPS * BLOCK, LANES), f32),
            V((TIPS, 8, LANES), f32),
            V((TIPS * 8, LANES), f32),
            V((TIPS, LANES), f32),
            V((2, LANES, LANES), f32),
            V((BLOCK * 32, LANES), f32),
            V((groups, BLOCK, 2 * LANES), bf16),
            V((8, LANES), f32),
            V((groups, 8, LANES), f32),
            V((LANES, LANES), f32),
            V((groups, 8, LANES), f32),
            V((groups, 8, LANES), f32),
            V((2, LANES, LANES), f32),
            V((8, LANES), f32),
            V((site_devs, 8, LANES), f32),
            D((groups,)), D((groups,)),
            D((groups,)), D((groups,)),
            D((groups,)), D((groups,)),
            D((site_devs,)), D((site_devs,)),
        ],
        compiler_params=pltpu.CompilerParams(
            collective_id=0, has_side_effects=True, vmem_limit_bytes=60 * 1024 * 1024
        ),
        cost_estimate=pl.CostEstimate(flops=312_000_000, bytes_accessed=200_000, transcendentals=200_000),
    )(tip_states, lens, parents, exchange, freqs.reshape(1, STATES), gamma_rates)
    return total[0:2].reshape(1, 256)[:, :254], total[1:2, 126:128]


def solution(mesh):
    in_specs = (P("leaf", "site"), P("leaf", None), P("leaf", None), P("leaf", None), P(), P(), P())
    out_specs = (P("leaf", None), P("leaf", None))
    return jax.shard_map(
        per_device, mesh=mesh, in_specs=in_specs, out_specs=out_specs, check_vma=False
    )
```

time: 773 us -> 64.1 us (0.08)
  the two profiles are of different devices: /device:TPU:96 before, /device:TPU:0 now
where the time goes in v1:
time: 64.1 us; the launch traced here: 63.8 us
  Pallas kernels  58.1 us (91%)
  local copies, waits for them, and re-layouts  4.41 us (7%)
  between operations  0.66 us (1%)
    pallas_call x1, Pallas kernels, per_device(): pl.pallas_call(kernel, out_shape=jax.ShapeDtypeStruct((8, LANES), f32), i...  58.1 us
    slice x2, local copies, waits for them, and re-layouts, per_device(): return (total[0:2].reshape(1, 256)[:, :254], total[1:2, 126:128])  2.5 us
    unnamed x6, local copies, waits for them, and re-layouts  1.36 us

profile of v1, /device:TPU:0, one launch (start us, length us, event | category | flops | bytes accessed | tf_op | source)
XLA Modules:
  0.0 63.8 jit_solution(14404286725746728756)
XLA Ops:
  0.6 0.0 copy-start.2
  0.6 0.0 copy-start
  0.6 0.6 copy-done.2
  1.3 0.0 copy-done
  1.3 0.6 pad_maximum_fusion
  2.0 0.0 copy-start.1
  2.0 0.7 %copy-done.1 = s32[1,254]{1,0:T(1,128)S(1)} copy-done((s32[1,254]{1,0:T(1,128)S(1)}, s32[1,254]{1,0:T(1,128)}, u32[]{:S(2)}) %copy-start.1) | copy-done | bytes 1040
  2.6 0.5 concatenate.7
  3.2 58.1 %shard_map.86 = f32[8,128]{1,0:T(8,128)} custom-call(s32[128,128]{1,0:T(8,128)} %tips_ref.1, f32[2,128]{1,0:T(2,128)} %bitcast.6, s32[2,128]{1,0:T(2,128)} %bitcast.7, f32[20,20]{1,0:T(8,128)} %exchange_ref.1, f32[1,20]{1,0:T(1,128)} %bitcast.8, f32[4]{0:T(128)} %gamma_ref.1), custom_call_target="tpu_custom_call" | custom-call | flops 312000000 | bytes 200000 | tf_op jit(solution)/shard_map/pallas_call | solution.py:513
  61.3 1.3 %slice.11 = f32[1,2]{1,0:T(1,128)} slice(f32[8,128]{1,0:T(8,128)} %shard_map.86), slice={[1:2], [126:128]} | slice | bytes 16 | tf_op jit(solution)/shard_map/slice | solution.py:558
  62.6 1.2 %slice.9 = f32[2,128]{1,0:T(2,128)} slice(f32[8,128]{1,0:T(8,128)} %shard_map.86), slice={[0:2], [0:128]} | slice | bytes 2048 | tf_op jit(solution)/shard_map/slice | solution.py:558
Async XLA Ops:
  0.6 0.7 %copy-start.2 = (f32[1,2]{1,0:T(1,128)S(1)}, f32[1,2]{1,0:T(1,128)}, u32[]{:S(2)}) copy-start(f32[1,2]{1,0:T(1,128)} %param.9) | copy-start | bytes 28
  0.6 0.7 %copy-start = (f32[1,254]{1,0:T(1,128)S(1)}, f32[1,254]{1,0:T(1,128)}, u32[]{:S(2)}) copy-start(f32[1,254]{1,0:T(1,128)} %param.8) | copy-start | bytes 3052
  2.0 0.7 %copy-start.1 = (s32[1,254]{1,0:T(1,128)S(1)}, s32[1,254]{1,0:T(1,128)}, u32[]{:S(2)}) copy-start(s32[1,254]{1,0:T(1,128)} %param.10) | copy-start | bytes 3052

commit v2 on v1

v2 whole, which is shorter than its diff:
```python
import math

import jax
import jax.numpy as jnp
from jax import lax
from jax.experimental import pallas as pl
from jax.experimental.pallas import tpu as pltpu
from jax.sharding import PartitionSpec as P

STATES = 20
RATES = 4
TERMS = 16
TIPS = 128
BLOCK = STATES * RATES
LANES = 128
MESH = pl.DeviceIdType.MESH
LEVEL_BASE = (0, 64, 96, 112, 120, 124, 126)

f32 = jnp.float32
bf16 = jnp.bfloat16
i32 = jnp.int32


def iota(shape, dim):
    return lax.broadcasted_iota(i32, shape, dim)


def lookup(table, index):
    return jnp.take_along_axis(table, index, axis=1, mode="promise_in_bounds")


def dot(a, b):
    return jnp.dot(a, b, preferred_element_type=f32)


def halves(x):
    high = x.astype(bf16)
    return high, (x - high.astype(f32)).astype(bf16)


def staircase(lane, starts, values):
    out = jnp.full(lane.shape, values[0], i32)
    for start, value in zip(starts[1:], values[1:]):
        out = jnp.where(lane >= start, value, out)
    return out


def category_of(position):
    return jnp.where(position < 64, position >> 4, (position - 64) >> 2)


def state_of(position):
    return jnp.where(position < 64, position & 15, 16 + (position & 3))


def pack_vector(high, low):
    return jnp.concatenate([high, low, high, jnp.zeros((16, LANES), bf16)], axis=0)


def kernel(
    tips_ref, local_ref, upper_ref, parents_ref, exchange_ref, freqs_ref, gamma_ref, local_out, upper_out,
    rows_f, rows_i, pad, plain, spread0, spread1, pi_rows, masks, made_w, tip_table, table0, table1, packed,
    tip_pos, partial, parts, tip_message, tip_slope, message, slope, norm, acc, place,
    chain_src, chain_all, chain_rhs, lift_t, lift_all, z_out, z_in, sum_src, sum_all,
    chain_send, chain_recv, lift_send, lift_recv, z_send, z_recv, sum_send, sum_recv,
):
    me = lax.axis_index("leaf")
    site = lax.axis_index("site")
    groups = lax.axis_size("leaf")
    site_devs = lax.axis_size("site")
    spread = (spread0, spread1)
    table = (table0, table1)
    above = partial

    def leaf_peer(offset):
        return lax.rem(me + offset, groups)

    core, x_at, z_at = lax.rem(me, 2), lax.rem(me // 2, 4), me // 8
    steps = [(dz, dx, dc) for dz in range(4) for dx in range(4) for dc in range(2)][1:]
    steps.sort(key=lambda d: -(min(d[0], 4 - d[0]) + min(d[1], 4 - d[1])))
    peers = [
        lax.rem(z_at + dz, 4) * 8 + lax.rem(x_at + dx, 4) * 2 + lax.rem(core + dc, 2) for dz, dx, dc in steps
    ]

    barrier = pltpu.get_barrier_semaphore()

    def greet_leaf(offset, carry):
        pl.semaphore_signal(barrier, inc=1, device_id=(leaf_peer(offset), site), device_id_type=MESH)
        return carry

    def greet_site(offset, carry):
        pl.semaphore_signal(
            barrier, inc=1, device_id=(me, lax.rem(site + offset, site_devs)), device_id_type=MESH
        )
        return carry

    lax.fori_loop(1, groups, greet_leaf, 0)
    lax.fori_loop(1, site_devs, greet_site, 0)

    lane = iota((8, LANES), 1)[:1]
    square_lane = iota((LANES, LANES), 1)
    square_row = iota((LANES, LANES), 0)

    rows_i[...] = jnp.zeros_like(rows_i)
    rows_i[1:2, 0:126] = parents_ref[0:1, 128:254]
    rows_f[...] = jnp.ones_like(rows_f)
    rows_f[1:2, 0:126] = local_ref[0:1, 128:254]
    rows_f[1:2, 126:128] = upper_ref[...]
    tip_parent = parents_ref[0:1, 0:128]
    raw_parent = rows_i[1:2, :]
    own_base = staircase(lane, LEVEL_BASE, LEVEL_BASE)
    next_base = staircase(lane, LEVEL_BASE, LEVEL_BASE[1:] + (126,))
    half = staircase(lane, LEVEL_BASE, (32, 16, 8, 4, 2, 1, 0))
    is_node = lane < 126
    node_parent = jnp.where(is_node, raw_parent + next_base, lane)

    def second_child(parent_row):
        across = jnp.broadcast_to(parent_row.astype(f32), (LANES, LANES))
        down = jnp.transpose(across)
        hit = (across == down) & (square_row < square_lane)
        return jnp.max(jnp.where(hit, 1.0, 0.0), axis=0, keepdims=True).astype(i32)

    node_second = second_child(jnp.where(is_node, node_parent, lane + 200))
    tip_second = second_child(tip_parent)
    position = lane
    for _ in range(6):
        found = lookup(jnp.broadcast_to(position, (8, LANES)), jnp.broadcast_to(node_parent, (8, LANES)))[:1]
        position = jnp.where(is_node, own_base + node_second * half + found - next_base, lane)
    found = lookup(jnp.broadcast_to(position, (8, LANES)), jnp.broadcast_to(tip_parent, (8, LANES)))[:1]
    tip_position = tip_second * 64 + found
    tip_place = jnp.where(square_row == tip_position, 1.0, 0.0)
    node_place = jnp.where(square_row == position, 1.0, 0.0)
    place[0] = tip_place
    place[1] = node_place
    tip_pos[...] = dot(tip_place.astype(bf16), tips_ref[...].astype(f32).astype(bf16)).astype(i32)
    tip_len = jnp.sum(tip_place * local_ref[0:1, 0:128], axis=1, keepdims=True)
    node_len = jnp.sum(node_place * rows_f[1:2, :], axis=1, keepdims=True)

    columns = []
    for tile in range(2):
        at = lane + LANES * tile
        at = jnp.where(at >= 240, -1, jnp.where(at >= 160, at - 160, jnp.where(at >= 80, at - 80, at)))
        columns.append(at)
        cat = jnp.broadcast_to(jnp.where(at < 0, -1, category_of(at)), (16, LANES))
        for c in range(RATES):
            masks[tile, c] = jnp.where(cat == c, 1.0, 0.0).astype(bf16)
        masks[tile, RATES] = jnp.where(cat == (iota((16, LANES), 0) >> 2), 1.0, 0.0).astype(bf16)
    inside = jnp.where(lane < BLOCK, 1.0, 0.0)
    for c in range(RATES + 1):
        masks[2, c] = (masks[0, c].astype(f32) * inside).astype(bf16)
    state_col = [jnp.where(at < 0, 0, state_of(at)) for at in columns]
    row80 = iota((BLOCK, LANES), 0)
    row_state = state_of(row80)
    left_state = jnp.where(category_of(row80) < 2, row_state, -1)
    right_state = jnp.where(category_of(row80) < 2, -1, row_state)
    lane_part = category_of(lane)

    pad[...] = jnp.zeros_like(pad)
    pad[0:20, 0:20] = exchange_ref[...]
    pad[24:25, 0:20] = freqs_ref[...]
    freqs = pad[24:25, :]
    pi_row = freqs / jnp.sum(freqs, axis=1, keepdims=True)
    row24 = iota((24, LANES), 0)
    lane24 = iota((24, LANES), 1)
    eye = jnp.where((row24 == lane24) & (row24 < STATES), 1.0, 0.0)
    off = pad[0:24, :] * pi_row * (1.0 - eye)
    outflow = jnp.sum(off, axis=1, keepdims=True)
    pi_col = jnp.sum(eye * pi_row, axis=1, keepdims=True)
    overall = jnp.sum(pi_col * outflow, axis=0, keepdims=True)
    fastest = jnp.max(outflow, axis=0, keepdims=True)
    uniform = fastest / overall
    step = eye + (off - eye * outflow) / fastest
    pi_bcast = jnp.broadcast_to(pi_col, (24, LANES))
    pi_rows[...] = pi_bcast
    pi80 = jnp.concatenate([pi_bcast[0:16]] * 4 + [pi_bcast[16:20]] * 4, axis=0)

    def spread_columns(x):
        return [
            jnp.concatenate(
                [lookup(x[8 * k : 8 * k + 8], jnp.broadcast_to(state_col[tile], (8, LANES))) for k in range(3)], axis=0
            )
            for tile in range(2)
        ]

    rest = jnp.zeros((104, 3 * LANES), f32)

    def advance(rows, by):
        operand = jnp.concatenate([by] + spread_columns(by), axis=1)
        operand = jnp.concatenate([operand, rest], axis=0)
        return jnp.dot(rows, operand, precision=lax.Precision.HIGHEST, preferred_element_type=f32)

    def keep_spread(power, tiles):
        for tile in range(2):
            high = tiles[tile].astype(bf16).astype(f32)
            low = tiles[tile] - high
            for term, value in enumerate((high, low, high)):
                u = 21 * term + power
                spread[tile][24 * u : 24 * u + 24, :] = value

    def keep_powers(start, made):
        count = made.shape[0] // 24
        plain[24 * start : 24 * (start + count), :] = made[:, :LANES]
        for k in range(count):
            rows = made[24 * k : 24 * k + 24]
            keep_spread(start + k, [rows[:, LANES : 2 * LANES], rows[:, 2 * LANES :]])

    for u in (17, 18, 19, 20, 38, 39, 40, 41, 59, 60, 61, 62, 63):
        for tile in range(2):
            spread[tile][24 * u : 24 * u + 24, :] = jnp.zeros((24, LANES), f32)
    keep_spread(0, spread_columns(eye))
    keep_spread(1, spread_columns(step))
    plain[24:48, :] = step
    second = advance(step, step)
    keep_powers(2, second)
    upto4 = advance(plain[24:72, :], second[:, :LANES])
    keep_powers(3, upto4)
    upto8 = advance(plain[24:120, :], upto4[24:48, :LANES])
    keep_powers(5, upto8)
    keep_powers(9, advance(plain[24:216, :], upto8[72:96, :LANES]))

    within = lane & 63
    term = jnp.where(within >= 42, 2, jnp.where(within >= 21, 1, 0))
    power = within - 21 * term
    power_f = power.astype(f32)
    log_factorial = jnp.zeros((1, LANES), f32)
    for m in range(2, TERMS + 1):
        log_factorial = log_factorial + jnp.where(power >= m, math.log(m), 0.0)

    def lay(value):
        high = value.astype(bf16).astype(f32)
        return jnp.where(term < 2, high, value - high).astype(bf16)

    for which, column in enumerate((tip_len, node_len)):
        lengths = jnp.broadcast_to(column, (TIPS, LANES))
        log_lengths = jnp.log(lengths)
        per_length = power_f / lengths
        for tile in range(2):
            speed = jnp.where(lane < 64, gamma_ref[2 * tile], gamma_ref[2 * tile + 1]) * uniform
            w = jnp.exp(power_f * (log_lengths + jnp.log(speed)) - lengths * speed - log_factorial)
            w = jnp.where(power <= TERMS, w, 0.0)
            at = slice(LANES * tile, LANES * (tile + 1))
            made_w[0, TIPS * which : TIPS * (which + 1), at] = lay(w)
            made_w[1, TIPS * which : TIPS * (which + 1), at] = lay(w * (per_length - speed))

    def table_row(kind, i, octet, r):
        base = [spread[tile][pl.ds(i, 64, stride=24), :].astype(bf16) for tile in range(2)]
        tiles = [
            jnp.concatenate(
                [base[tile] * jnp.concatenate([masks[tile, c]] * 4, axis=0) for c in range(RATES)], axis=0
            )
            for tile in range(2)
        ]
        made = dot(made_w[kind, TIPS:, :], jnp.concatenate(tiles, axis=1))
        blank = jnp.zeros((64, LANES), bf16)
        two = jnp.concatenate(
            [jnp.concatenate([base[0], blank], axis=1), jnp.concatenate([blank, base[0]], axis=1)], axis=0
        )
        tip_made = [dot(made_w[kind, :TIPS, LANES * k : LANES * (k + 1)], two) for k in range(2)]
        if kind:
            scale = pi_rows[pl.ds(i, 1), :]
            scale = jnp.concatenate([scale, scale], axis=1)
            made = made * scale
            tip_made = [x * scale for x in tip_made]
        start = (3 * kind + octet) * 8 * TIPS
        for tile in range(2):
            value = made[:, LANES * tile : LANES * (tile + 1)]
            table[tile][pl.ds(start + r, TIPS, stride=8), :] = value
            if octet == 2:
                table[tile][pl.ds(start + r + 4, TIPS, stride=8), :] = value
        for c in range(RATES):
            value = tip_made[c // 2][:, LANES * (c % 2) : LANES * (c % 2 + 1)]
            if octet == 2:
                row = (8 + c // 2) * 8 * TIPS + 4 * (c % 2) + r
            else:
                row = (2 * c + octet) * 8 * TIPS + r
            tip_table[pl.ds(row, TIPS, stride=8), :] = value

    def build_tables(kind):
        for octet in range(2):

            def rows(turn, carry):
                for part in range(2):
                    r = 2 * turn + part
                    table_row(kind, 8 * octet + r, octet, r)
                return carry

            lax.fori_loop(0, 4, rows, 0)

        def last_rows(turn, carry):
            for part in range(2):
                r = 2 * turn + part
                table_row(kind, 16 + r, 2, r)
            return carry

        lax.fori_loop(0, 2, last_rows, 0)

    def read_table(tile, kind, node):
        start = kind * 3 * 8 * TIPS
        return [
            table[tile][pl.ds(pl.multiple_of(start + 8 * TIPS * k + 8 * node, 8), 8), :] for k in range(3)
        ]

    def blocks(octets, tile):
        upper = jnp.concatenate(octets[:2], axis=0).astype(bf16)
        last = jnp.concatenate([octets[2]] * 2, axis=0).astype(bf16)
        return jnp.concatenate(
            [upper * masks[tile, c] for c in range(RATES)] + [last * masks[tile, RATES]], axis=0
        )

    def pack_matrix(kind, node):
        left = blocks(read_table(0, kind, node), 0)
        octets = []
        for x in read_table(1, kind, node):
            octets.append(jnp.where(lane < 32, x, x - x.astype(bf16).astype(f32)))
        return jnp.concatenate([left, blocks(octets, 1)], axis=1)

    build_tables(0)

    pl.semaphore_wait(barrier, groups - 1 + site_devs - 1)
    own_chain = jnp.concatenate(read_table(0, 0, 127), axis=0)
    chain_src[...] = own_chain
    chain_all[me] = own_chain

    for peer in peers:
        pltpu.make_async_remote_copy(
            src_ref=chain_src, dst_ref=chain_all.at[me], send_sem=chain_send, recv_sem=chain_recv,
            device_id=(peer, site), device_id_type=MESH,
        ).start()

    def wait_all(ref, sem):
        pltpu.make_async_copy(ref, ref, sem).wait()

    def tip_pair(m):
        rows = []
        for octet in range(10):
            at = octet * 8 * TIPS
            left = tip_table[pl.ds(pl.multiple_of(at + 8 * m, 8), 8), :]
            right = tip_table[pl.ds(pl.multiple_of(at + 8 * m + 512, 8), 8), :]
            rows.append(jnp.where(lane_part < 2, left, right))
        x = jnp.concatenate(rows, axis=0)
        x = jnp.where(lane_part % 2 == 0, x, x - x.astype(bf16).astype(f32)).astype(bf16)
        left = jnp.broadcast_to(tip_pos[pl.ds(m, 1), :], (BLOCK, LANES)) == left_state
        right = jnp.broadcast_to(tip_pos[pl.ds(m + 64, 1), :], (BLOCK, LANES)) == right_state
        operand = jnp.concatenate([jnp.where(left, 1.0, 0.0), jnp.where(right, 1.0, 0.0)], axis=1)
        made = dot(x[:, :BLOCK], operand.astype(bf16))
        return made[:, :LANES], made[:, LANES:]

    def tips_up(turn, carry):
        for part in range(8):
            m = turn * 8 + part
            left, right = tip_pair(m)
            tip_message[m] = left
            tip_message[m + 64] = right
            partial[m] = left * right
        return carry

    lax.fori_loop(0, 8, tips_up, 0)

    def node_up(node):
        matrix = pack_matrix(0, node)
        packed[node] = matrix
        high, low = halves(partial[node])
        parts[node, 0:BLOCK] = high
        parts[node, BLOCK:] = low
        made = dot(matrix, pack_vector(high, low))
        message[node] = made
        return made

    for level in range(1, 7):
        base, after = LEVEL_BASE[level - 1], LEVEL_BASE[level]
        pairs = 64 >> level
        batch = min(pairs, 8)

        def pairs_up(turn, carry):
            for part in range(batch):
                m = turn * batch + part
                product = node_up(base + m) * node_up(base + pairs + m)
                factor = 1.0 / jnp.max(product, axis=0, keepdims=True)
                norm[after + m] = jnp.broadcast_to(factor, (8, LANES))
                partial[after + m] = product * factor
            return carry

        lax.fori_loop(0, pairs // batch, pairs_up, 0)

    lifted = node_up(126)

    lift_t[...] = jnp.transpose(jnp.concatenate([lifted, jnp.zeros((LANES - BLOCK, LANES), f32)], axis=0))
    pair_no = me // 2
    side = lax.rem(me, 2)
    lift_all[me] = lift_t[pl.ds(pl.multiple_of(8 * pair_no, 8), 8), :]

    for peer in peers:
        pltpu.make_async_remote_copy(
            src_ref=lift_t.at[pl.ds(pl.multiple_of(8 * (peer // 2), 8), 8), :], dst_ref=lift_all.at[me],
            send_sem=lift_send, recv_sem=lift_recv, device_id=(peer, site), device_id_type=MESH,
        ).start()

    build_tables(1)

    def tips_slope(turn, carry):
        for part in range(8):
            m = turn * 8 + part
            left, right = tip_pair(m)
            tip_slope[m] = left
            tip_slope[m + 64] = right
        return carry

    lax.fori_loop(0, 8, tips_slope, 0)

    wait_all(chain_all.at[0 : groups - 1], chain_recv)

    def chain_pack(g, carry):
        x = chain_all[g]
        high = x.astype(bf16).astype(f32)
        for tile, value in enumerate((high, x - high)):
            chain_rhs[g, :, LANES * tile : LANES * (tile + 1)] = blocks([value[0:8], value[8:16], value[16:24]], 2)
        return carry

    lax.fori_loop(0, groups, chain_pack, 0)

    wait_all(lift_all.at[0 : groups - 1], lift_recv)

    pi_lanes = lookup(jnp.broadcast_to(pi_row, (8, LANES)), jnp.broadcast_to(state_col[0], (8, LANES))) * inside
    is_up = side == 0
    own_rows = pl.ds(pl.multiple_of(LANES * side + 8 * pair_no, 8), 8)

    def chain_step(t, z):
        g = jnp.where(is_up, t, groups - 1 - t)
        z_out[g] = z

        @pl.when(g != me)
        def _():
            pltpu.make_async_remote_copy(
                src_ref=z_out.at[g], dst_ref=z_in.at[own_rows, :], send_sem=z_send, recv_sem=z_recv,
                device_id=(g, site), device_id_type=MESH,
            ).start()

        lift = lift_all[g]
        before = jnp.where(is_up, lift, 1.0) * z
        factor = jnp.where(is_up, 1.0, lift) / jnp.max(before, axis=1, keepdims=True)
        high, low = halves(before)
        made = dot(jnp.concatenate([high, low], axis=0)[:, :BLOCK], chain_rhs[g])
        return (made[0:8, :LANES] + (made[8:16, :LANES] + made[0:8, LANES:])) * factor

    lax.fori_loop(0, groups, chain_step, pi_lanes)
    z_in[own_rows, :] = z_out[me]

    def node_slope(node):
        slope[node] = dot(pack_matrix(1, node), pack_vector(parts[node, 0:BLOCK], parts[node, BLOCK:]))

    def nodes_slope(turn, carry):
        for part in range(14):
            node_slope(turn * 14 + part)
        return carry

    lax.fori_loop(0, 9, nodes_slope, 0)
    node_slope(126)

    wait_all(z_in.at[0 : 8 * (groups - 1)], z_recv)

    below = jnp.transpose(z_in[0:LANES])[:BLOCK] / pi80
    outside = jnp.transpose(z_in[LANES:])[:BLOCK] / pi80
    lifted = message[126]
    beside = dot(pack_matrix(0, 127), pack_vector(*halves(outside))) * below
    scale = 1.0 / jnp.max(beside, axis=0, keepdims=True)
    beside = beside * scale
    outside = outside * scale
    scale = 1.0 / jnp.sum(pi80 * beside * lifted, axis=0, keepdims=True)
    beside = beside * scale
    outside = outside * scale
    chain_slope = dot(pack_matrix(1, 127), pack_vector(*halves(lifted * below)))

    def fold(x):
        total = x[0:8]
        for k in range(1, BLOCK // 8):
            total = total + x[8 * k : 8 * k + 8]
        return total

    def keep_acc(node, x):
        acc[pl.ds(pl.multiple_of(8 * node, 8), 8), :] = fold(x)

    keep_acc(TIPS + 127, outside * chain_slope)

    def node_down(node, pre):
        keep_acc(TIPS + node, pre * slope[node])
        above[node] = dot(packed[node], pack_vector(*halves(pre)))

    node_down(126, beside)

    for level in range(6, 0, -1):
        base, after = LEVEL_BASE[level - 1], LEVEL_BASE[level]
        pairs = 64 >> level
        batch = min(pairs, 8)

        def pairs_down(turn, carry):
            for part in range(batch):
                m = turn * batch + part
                left, right = base + m, base + pairs + m
                over = above[after + m] * norm[after + m][:1]
                node_down(left, over * message[right])
                node_down(right, over * message[left])
            return carry

        lax.fori_loop(0, pairs // batch, pairs_down, 0)

    def tips_down(turn, carry):
        for part in range(2):
            m = turn * 2 + part
            over = above[m]
            keep_acc(m, over * tip_message[m + 64] * tip_slope[m])
            keep_acc(m + 64, over * tip_message[m] * tip_slope[m + 64])
        return carry

    lax.fori_loop(0, 32, tips_down, 0)

    def total_of(which):
        start = 8 * TIPS * which
        folded = acc[pl.ds(start, TIPS, stride=8), :]
        for k in range(1, 8):
            folded = folded + acc[pl.ds(start + k, TIPS, stride=8), :]
        return jnp.sum(place[which] * jnp.sum(folded, axis=1, keepdims=True), axis=0, keepdims=True)

    share = jnp.concatenate([total_of(0), total_of(1), jnp.zeros((6, LANES), f32)], axis=0)
    share = share * (1.0 / (LANES * site_devs))
    sum_src[...] = share
    sum_all[site] = share
    for offset in range(1, site_devs):
        pltpu.make_async_remote_copy(
            src_ref=sum_src, dst_ref=sum_all.at[site], send_sem=sum_send, recv_sem=sum_recv,
            device_id=(me, lax.rem(site + offset, site_devs)), device_id_type=MESH,
        ).start()
    wait_all(sum_all.at[0 : site_devs - 1], sum_recv)
    total = sum_all[0]
    for k in range(1, site_devs):
        total = total + sum_all[k]
    local_out[:, 0:128] = total[0:1]
    local_out[:, 128:254] = total[1:2, :126]
    upper_out[...] = total[1:2, 126:128]
    wait_all(chain_all.at[0 : groups - 1], chain_send)
    wait_all(lift_all.at[0 : groups - 1], lift_send)
    wait_all(z_out.at[0 : groups - 1], z_send)
    wait_all(sum_all.at[0 : site_devs - 1], sum_send)


def per_device(tip_states, local_len, upper_len, parent_lists, exchange, freqs, gamma_rates):
    groups = lax.axis_size("leaf")
    site_devs = lax.axis_size("site")
    vmem = pl.BlockSpec(memory_space=pltpu.VMEM)
    smem = pl.BlockSpec(memory_space=pltpu.SMEM)
    V = pltpu.VMEM
    D = pltpu.SemaphoreType.DMA
    return pl.pallas_call(
        kernel,
        out_shape=(jax.ShapeDtypeStruct((1, 254), f32), jax.ShapeDtypeStruct((1, 2), f32)),
        in_specs=[vmem] * 6 + [smem],
        out_specs=(vmem, vmem),
        scratch_shapes=[
            V((8, LANES), f32), V((8, LANES), i32),
            V((32, LANES), f32),
            V((17 * 24, LANES), f32),
            V((64 * 24, LANES), f32), V((64 * 24, LANES), f32),
            V((24, LANES), f32),
            V((3, RATES + 1, 16, LANES), bf16),
            V((2, 2 * TIPS, 2 * LANES), bf16),
            V((BLOCK * TIPS, LANES), f32),
            V((2 * 3 * 8 * TIPS, LANES), f32), V((2 * 3 * 8 * TIPS, LANES), f32),
            V((TIPS, BLOCK, 2 * LANES), bf16),
            V((TIPS, LANES), i32),
            V((TIPS, BLOCK, LANES), f32),
            V((TIPS, 2 * BLOCK, LANES), bf16),
            V((TIPS, BLOCK, LANES), f32),
            V((TIPS, BLOCK, LANES), f32),
            V((TIPS, BLOCK, LANES), f32),
            V((TIPS, BLOCK, LANES), f32),
            V((TIPS, 8, LANES), f32),
            V((2 * TIPS * 8, LANES), f32),
            V((2, LANES, LANES), f32),
            V((24, LANES), f32),
            V((groups, 24, LANES), f32),
            V((groups, BLOCK, 2 * LANES), bf16),
            V((LANES, LANES), f32),
            V((groups, 8, LANES), f32),
            V((groups, 8, LANES), f32),
            V((2 * LANES, LANES), f32),
            V((8, LANES), f32),
            V((site_devs, 8, LANES), f32),
            D, D, D, D, D, D, D, D,
        ],
        compiler_params=pltpu.CompilerParams(
            collective_id=0, has_side_effects=True, vmem_limit_bytes=60 * 1024 * 1024
        ),
        cost_estimate=pl.CostEstimate(flops=312_000_000, bytes_accessed=200_000, transcendentals=200_000),
    )(tip_states, local_len, upper_len, parent_lists, exchange, freqs.reshape(1, STATES), gamma_rates)


def solution(mesh):
    in_specs = (P("leaf", "site"), P("leaf", None), P("leaf", None), P("leaf", None), P(), P(), P())
    out_specs = (P("leaf", None), P("leaf", None))
    return jax.shard_map(
        per_device, mesh=mesh, in_specs=in_specs, out_specs=out_specs, check_vma=False
    )
```

time: 64.1 us -> 44.5 us (0.69)
  Pallas kernels: 58.1 us -> 41.8 us
  local copies, waits for them, and re-layouts: 4.41 us -> 1.8 us
    pallas_call x1, Pallas kernels: 58.1 us -> 41.8 us  [per_device(): pl.pallas_call(kernel, out_shape=(jax.ShapeDtypeStruct((1, 254), f32), ja...]
    slice x2 -> x0, local copies, waits for them, and re-layouts: 2.5 us -> none  [per_device(): return (total[0:2].reshape(1, 256)[:, :254], total[1:2, 126:128])]
where the time goes in v2:
time: 44.5 us; the launch traced here: 44.3 us
  Pallas kernels  41.8 us (94%)
  local copies, waits for them, and re-layouts  1.8 us (4%)
  between operations  0.65 us (1%)
    pallas_call x1, Pallas kernels, per_device(): pl.pallas_call(kernel, out_shape=(jax.ShapeDtypeStruct((1, 254), f32), ja...  41.8 us
    unnamed x6, local copies, waits for them, and re-layouts  1.8 us

profile of v2, /device:TPU:0, one launch (start us, length us, event | category | flops | bytes accessed | tf_op | source)
XLA Modules:
  0.0 44.3 jit_solution(6611926879729270508)
XLA Ops:
  0.6 41.8 %shard_map.86 = (f32[1,254]{1,0:T(1,128)}, f32[1,2]{1,0:T(1,128)}) custom-call(s32[128,128]{1,0:T(8,128)} %tips_ref.1, f32[1,254]{1,0:T(1,128)} %local_ref.1, f32[1,2]{1,0:T(1,128)} %upper_ref.1, s32[1,254]{1,0:T(1,128)} %parents_ref.1, f32[20,20]{1,0:T(8,128)} %exchange_ref.1, f32[1,20]{1,0:T(1,128)} %bitcast.1, f32[4]{0:T(128)} %gamma_ref.1), custom_call_target="tpu_custom_call" | custom-call | flops 312000000 | bytes 200000 | tf_op jit(solution)/shard_map/pallas_call | solution.py:552
  42.5 0.0 copy-start
  42.5 0.7 %copy-done = f32[1,254]{1,0:T(1,128)S(1)} copy-done((f32[1,254]{1,0:T(1,128)S(1)}, f32[1,254]{1,0:T(1,128)}, u32[]{:S(2)}) %copy-start) | copy-done | bytes 1040
  43.1 0.0 copy-start.1
  43.1 0.6 %copy.11 = f32[1,254]{1,0:T(1,128)} copy(f32[1,254]{1,0:T(1,128)S(1)} %copy-done) | data formatting | bytes 2032
  43.7 0.1 copy-done.1
  43.8 0.5 %copy.12 = f32[1,2]{1,0:T(1,128)} copy(f32[1,2]{1,0:T(1,128)S(1)} %copy-done.1) | data formatting | bytes 16
Async XLA Ops:
  42.5 0.7 %copy-start = (f32[1,254]{1,0:T(1,128)S(1)}, f32[1,254]{1,0:T(1,128)}, u32[]{:S(2)}) copy-start(f32[1,254]{1,0:T(1,128)} %get-tuple-element.4) | copy-start | bytes 3052
  43.1 0.6 %copy-start.1 = (f32[1,2]{1,0:T(1,128)S(1)}, f32[1,2]{1,0:T(1,128)}, u32[]{:S(2)}) copy-start(f32[1,2]{1,0:T(1,128)} %get-tuple-element.5) | copy-start | bytes 28

commit v3 on v2

--- a/solution.py
+++ b/solution.py
@@ -59,8 +59,8 @@
 
 def kernel(
     tips_ref, local_ref, upper_ref, parents_ref, exchange_ref, freqs_ref, gamma_ref, local_out, upper_out,
-    rows_f, rows_i, pad, plain, spread0, spread1, pi_rows, masks, made_w, tip_table, table0, table1, packed,
-    tip_pos, partial, parts, tip_message, tip_slope, message, slope, norm, acc, place,
+    rows_f, rows_i, pad, plain, spread0, spread1, pi_rows, masks, tip_w, node_w, tip_table, table0, table1, packed,
+    tip_pos, partial, tip_message, tip_slope, message, slope, norm, acc, place,
     chain_src, chain_all, chain_rhs, lift_t, lift_all, z_out, z_in, sum_src, sum_all,
     chain_send, chain_recv, lift_send, lift_recv, z_send, z_recv, sum_send, sum_recv,
 ):
@@ -84,18 +84,12 @@
 
     barrier = pltpu.get_barrier_semaphore()
 
-    def greet_leaf(offset, carry):
-        pl.semaphore_signal(barrier, inc=1, device_id=(leaf_peer(offset), site), device_id_type=MESH)
-        return carry
-
-    def greet_site(offset, carry):
+    for peer in peers:
+        pl.semaphore_signal(barrier, inc=1, device_id=(peer, site), device_id_type=MESH)
+    for offset in range(1, site_devs):
         pl.semaphore_signal(
             barrier, inc=1, device_id=(me, lax.rem(site + offset, site_devs)), device_id_type=MESH
         )
-        return carry
-
-    lax.fori_loop(1, groups, greet_leaf, 0)
-    lax.fori_loop(1, site_devs, greet_site, 0)
 
     lane = iota((8, LANES), 1)[:1]
     square_lane = iota((LANES, LANES), 1)
@@ -230,17 +224,24 @@
         high = value.astype(bf16).astype(f32)
         return jnp.where(term < 2, high, value - high).astype(bf16)
 
-    for which, column in enumerate((tip_len, node_len)):
-        lengths = jnp.broadcast_to(column, (TIPS, LANES))
+    def series(lengths, speeds):
         log_lengths = jnp.log(lengths)
         per_length = power_f / lengths
-        for tile in range(2):
-            speed = jnp.where(lane < 64, gamma_ref[2 * tile], gamma_ref[2 * tile + 1]) * uniform
+        made = []
+        for speed in speeds:
             w = jnp.exp(power_f * (log_lengths + jnp.log(speed)) - lengths * speed - log_factorial)
             w = jnp.where(power <= TERMS, w, 0.0)
-            at = slice(LANES * tile, LANES * (tile + 1))
-            made_w[0, TIPS * which : TIPS * (which + 1), at] = lay(w)
-            made_w[1, TIPS * which : TIPS * (which + 1), at] = lay(w * (per_length - speed))
+            made.append((lay(w), lay(w * (per_length - speed))))
+        return made
+
+    speeds = [gamma_ref[c] * uniform for c in range(RATES)]
+    for c, both in enumerate(series(jnp.where(lane < 64, tip_len[:64], tip_len[64:]), speeds)):
+        for kind in range(2):
+            tip_w[kind, :, LANES * c : LANES * (c + 1)] = both[kind]
+    tile_speeds = [jnp.where(lane < 64, speeds[2 * tile], speeds[2 * tile + 1]) for tile in range(2)]
+    for tile, both in enumerate(series(jnp.broadcast_to(node_len, (TIPS, LANES)), tile_speeds)):
+        for kind in range(2):
+            node_w[kind, :, LANES * tile : LANES * (tile + 1)] = both[kind]
 
     def table_row(kind, i, octet, r):
         base = [spread[tile][pl.ds(i, 64, stride=24), :].astype(bf16) for tile in range(2)]
@@ -250,12 +251,15 @@
             )
             for tile in range(2)
         ]
-        made = dot(made_w[kind, TIPS:, :], jnp.concatenate(tiles, axis=1))
-        blank = jnp.zeros((64, LANES), bf16)
+        made = dot(node_w[kind], jnp.concatenate(tiles, axis=1))
+        left = base[0] * jnp.concatenate([masks[0, 0] + masks[0, 1]] * 4, axis=0)
+        right = base[0] * jnp.concatenate([masks[0, 2] + masks[0, 3]] * 4, axis=0)
+        pair = jnp.concatenate([left, right], axis=0)
+        blank = jnp.zeros((LANES, LANES), bf16)
         two = jnp.concatenate(
-            [jnp.concatenate([base[0], blank], axis=1), jnp.concatenate([blank, base[0]], axis=1)], axis=0
+            [jnp.concatenate([pair, blank], axis=1), jnp.concatenate([blank, pair], axis=1)], axis=0
         )
-        tip_made = [dot(made_w[kind, :TIPS, LANES * k : LANES * (k + 1)], two) for k in range(2)]
+        tip_made = [dot(tip_w[kind, :, 256 * k : 256 * (k + 1)], two) for k in range(2)]
         if kind:
             scale = pi_rows[pl.ds(i, 1), :]
             scale = jnp.concatenate([scale, scale], axis=1)
@@ -270,29 +274,24 @@
         for c in range(RATES):
             value = tip_made[c // 2][:, LANES * (c % 2) : LANES * (c % 2 + 1)]
             if octet == 2:
-                row = (8 + c // 2) * 8 * TIPS + 4 * (c % 2) + r
+                row = (8 + c // 2) * 8 * 64 + 4 * (c % 2) + r
             else:
-                row = (2 * c + octet) * 8 * TIPS + r
-            tip_table[pl.ds(row, TIPS, stride=8), :] = value
+                row = (2 * c + octet) * 8 * 64 + r
+            tip_table[pl.ds(row, 64, stride=8), :] = value
 
     def build_tables(kind):
         for octet in range(2):
 
             def rows(turn, carry):
-                for part in range(2):
-                    r = 2 * turn + part
+                for part in range(4):
+                    r = 4 * turn + part
                     table_row(kind, 8 * octet + r, octet, r)
                 return carry
 
-            lax.fori_loop(0, 4, rows, 0)
-
-        def last_rows(turn, carry):
-            for part in range(2):
-                r = 2 * turn + part
-                table_row(kind, 16 + r, 2, r)
-            return carry
-
-        lax.fori_loop(0, 2, last_rows, 0)
+            lax.fori_loop(0, 2, rows, 0)
+
+        for r in range(4):
+            table_row(kind, 16 + r, 2, r)
 
     def read_table(tile, kind, node):
         start = kind * 3 * 8 * TIPS
@@ -331,13 +330,9 @@
         pltpu.make_async_copy(ref, ref, sem).wait()
 
     def tip_pair(m):
-        rows = []
-        for octet in range(10):
-            at = octet * 8 * TIPS
-            left = tip_table[pl.ds(pl.multiple_of(at + 8 * m, 8), 8), :]
-            right = tip_table[pl.ds(pl.multiple_of(at + 8 * m + 512, 8), 8), :]
-            rows.append(jnp.where(lane_part < 2, left, right))
-        x = jnp.concatenate(rows, axis=0)
+        x = jnp.concatenate(
+            [tip_table[pl.ds(pl.multiple_of(512 * octet + 8 * m, 8), 8), :] for octet in range(10)], axis=0
+        )
         x = jnp.where(lane_part % 2 == 0, x, x - x.astype(bf16).astype(f32)).astype(bf16)
         left = jnp.broadcast_to(tip_pos[pl.ds(m, 1), :], (BLOCK, LANES)) == left_state
         right = jnp.broadcast_to(tip_pos[pl.ds(m + 64, 1), :], (BLOCK, LANES)) == right_state
@@ -346,30 +341,27 @@
         return made[:, :LANES], made[:, LANES:]
 
     def tips_up(turn, carry):
-        for part in range(8):
-            m = turn * 8 + part
+        for part in range(16):
+            m = turn * 16 + part
             left, right = tip_pair(m)
             tip_message[m] = left
             tip_message[m + 64] = right
             partial[m] = left * right
         return carry
 
-    lax.fori_loop(0, 8, tips_up, 0)
+    lax.fori_loop(0, 4, tips_up, 0)
 
     def node_up(node):
         matrix = pack_matrix(0, node)
         packed[node] = matrix
-        high, low = halves(partial[node])
-        parts[node, 0:BLOCK] = high
-        parts[node, BLOCK:] = low
-        made = dot(matrix, pack_vector(high, low))
+        made = dot(matrix, pack_vector(*halves(partial[node])))
         message[node] = made
         return made
 
     for level in range(1, 7):
         base, after = LEVEL_BASE[level - 1], LEVEL_BASE[level]
         pairs = 64 >> level
-        batch = min(pairs, 8)
+        batch = min(pairs, 16)
 
         def pairs_up(turn, carry):
             for part in range(batch):
@@ -397,15 +389,15 @@
 
     build_tables(1)
 
-    def tips_slope(turn, carry):
-        for part in range(8):
-            m = turn * 8 + part
-            left, right = tip_pair(m)
-            tip_slope[m] = left
-            tip_slope[m + 64] = right
+    def node_slope(node):
+        slope[node] = dot(pack_matrix(1, node), pack_vector(*halves(partial[node])))
+
+    def nodes_slope(turn, carry):
+        for part in range(14):
+            node_slope(turn * 14 + part)
         return carry
 
-    lax.fori_loop(0, 8, tips_slope, 0)
+    lax.fori_loop(0, 3, nodes_slope, 0)
 
     wait_all(chain_all.at[0 : groups - 1], chain_recv)
 
@@ -440,20 +432,17 @@
         factor = jnp.where(is_up, 1.0, lift) / jnp.max(before, axis=1, keepdims=True)
         high, low = halves(before)
         made = dot(jnp.concatenate([high, low], axis=0)[:, :BLOCK], chain_rhs[g])
+        for part in range(2):
+            m = 2 * t + part
+            left, right = tip_pair(m)
+            tip_slope[m] = left
+            tip_slope[m + 64] = right
         return (made[0:8, :LANES] + (made[8:16, :LANES] + made[0:8, LANES:])) * factor
 
     lax.fori_loop(0, groups, chain_step, pi_lanes)
     z_in[own_rows, :] = z_out[me]
 
-    def node_slope(node):
-        slope[node] = dot(pack_matrix(1, node), pack_vector(parts[node, 0:BLOCK], parts[node, BLOCK:]))
-
-    def nodes_slope(turn, carry):
-        for part in range(14):
-            node_slope(turn * 14 + part)
-        return carry
-
-    lax.fori_loop(0, 9, nodes_slope, 0)
+    lax.fori_loop(3, 9, nodes_slope, 0)
     node_slope(126)
 
     wait_all(z_in.at[0 : 8 * (groups - 1)], z_recv)
@@ -490,7 +479,7 @@
     for level in range(6, 0, -1):
         base, after = LEVEL_BASE[level - 1], LEVEL_BASE[level]
         pairs = 64 >> level
-        batch = min(pairs, 8)
+        batch = min(pairs, 16)
 
         def pairs_down(turn, carry):
             for part in range(batch):
@@ -551,7 +540,7 @@
     D = pltpu.SemaphoreType.DMA
     return pl.pallas_call(
         kernel,
-        out_shape=(jax.ShapeDtypeStruct((1, 254), f32), jax.ShapeDtypeStruct((1, 2), f32)),
+        out_shape=(V((1, 254), f32), V((1, 2), f32)),
         in_specs=[vmem] * 6 + [smem],
         out_specs=(vmem, vmem),
         scratch_shapes=[
@@ -561,13 +550,13 @@
             V((64 * 24, LANES), f32), V((64 * 24, LANES), f32),
             V((24, LANES), f32),
             V((3, RATES + 1, 16, LANES), bf16),
-            V((2, 2 * TIPS, 2 * LANES), bf16),
-            V((BLOCK * TIPS, LANES), f32),
+            V((2, 64, 4 * LANES), bf16),
+            V((2, TIPS, 2 * LANES), bf16),
+            V((BLOCK * 64, LANES), f32),
             V((2 * 3 * 8 * TIPS, LANES), f32), V((2 * 3 * 8 * TIPS, LANES), f32),
             V((TIPS, BLOCK, 2 * LANES), bf16),
             V((TIPS, LANES), i32),
             V((TIPS, BLOCK, LANES), f32),
-            V((TIPS, 2 * BLOCK, LANES), bf16),
             V((TIPS, BLOCK, LANES), f32),
             V((TIPS, BLOCK, LANES), f32),
             V((TIPS, BLOCK, LANES), f32),

time: 44.5 us -> 39.4 us (0.89)
  Pallas kernels: 41.8 us -> 37.5 us
  local copies, waits for them, and re-layouts: 1.8 us -> 1.07 us
    pallas_call x1, Pallas kernels: 41.8 us -> 37.5 us  [per_device(): pl.pallas_call(kernel, out_shape=(V((1, 254), f32), V((1, 2), f32)), in_s...]
    unnamed x6 -> x2, local copies, waits for them, and re-layouts: 1.8 us -> 1.07 us
where the time goes in v3:
time: 39.4 us; the launch traced here: 39.2 us
  Pallas kernels  37.5 us (95%)
  local copies, waits for them, and re-layouts  1.07 us (3%)
  between operations  0.64 us (2%)
    pallas_call x1, Pallas kernels, per_device(): pl.pallas_call(kernel, out_shape=(V((1, 254), f32), V((1, 2), f32)), in_s...  37.5 us
    unnamed x2, local copies, waits for them, and re-layouts  1.07 us

profile of v3, /device:TPU:0, one launch (start us, length us, event | category | flops | bytes accessed | tf_op | source)
XLA Modules:
  0.0 39.2 jit_solution(6751131811917100407)
XLA Ops:
  0.6 37.5 %shard_map.86 = (f32[1,254]{1,0:T(1,128)S(1)}, f32[1,2]{1,0:T(1,128)S(1)}) custom-call(s32[128,128]{1,0:T(8,128)} %tips_ref.1, f32[1,254]{1,0:T(1,128)} %local_ref.1, f32[1,2]{1,0:T(1,128)} %upper_ref.1, s32[1,254]{1,0:T(1,128)} %parents_ref.1, f32[20,20]{1,0:T(8,128)} %exchange_ref.1, f32[1,20]{1,0:T(1,128)} %bitcast.1, f32[4]{0:T(128)} %gamma_ref.1), custom_call_target="tpu_custom_call" | custom-call | flops 312000000 | bytes 200000 | tf_op jit(solution)/shard_map/pallas_call | solution.py:541
  38.2 0.6 %copy.11 = f32[1,254]{1,0:T(1,128)} copy(f32[1,254]{1,0:T(1,128)S(1)} %get-tuple-element.2) | data formatting | bytes 2032
  38.7 0.5 %copy.12 = f32[1,2]{1,0:T(1,128)} copy(f32[1,2]{1,0:T(1,128)S(1)} %get-tuple-element.3) | data formatting | bytes 16

commit v4 on v3

--- a/solution.py
+++ b/solution.py
@@ -58,7 +58,7 @@
 
 
 def kernel(
-    tips_ref, local_ref, upper_ref, parents_ref, exchange_ref, freqs_ref, gamma_ref, local_out, upper_out,
+    tips_ref, local_ref, upper_ref, parents_ref, exchange_ref, freqs_ref, gamma_ref, out_ref,
     rows_f, rows_i, pad, plain, spread0, spread1, pi_rows, masks, tip_w, node_w, tip_table, table0, table1, packed,
     tip_pos, partial, tip_message, tip_slope, message, slope, norm, acc, place,
     chain_src, chain_all, chain_rhs, lift_t, lift_all, z_out, z_in, sum_src, sum_all,
@@ -397,6 +397,17 @@
             node_slope(turn * 14 + part)
         return carry
 
+    def pair_slope(m):
+        left, right = tip_pair(m)
+        tip_slope[m] = left * tip_message[m + 64]
+        tip_slope[m + 64] = right * tip_message[m]
+
+    def pairs_slope(turn, carry):
+        for part in range(8):
+            pair_slope(turn * 8 + part)
+        return carry
+
+    lax.fori_loop(0, 4, pairs_slope, 0)
     lax.fori_loop(0, 3, nodes_slope, 0)
 
     wait_all(chain_all.at[0 : groups - 1], chain_recv)
@@ -432,16 +443,12 @@
         factor = jnp.where(is_up, 1.0, lift) / jnp.max(before, axis=1, keepdims=True)
         high, low = halves(before)
         made = dot(jnp.concatenate([high, low], axis=0)[:, :BLOCK], chain_rhs[g])
-        for part in range(2):
-            m = 2 * t + part
-            left, right = tip_pair(m)
-            tip_slope[m] = left
-            tip_slope[m + 64] = right
         return (made[0:8, :LANES] + (made[8:16, :LANES] + made[0:8, LANES:])) * factor
 
     lax.fori_loop(0, groups, chain_step, pi_lanes)
     z_in[own_rows, :] = z_out[me]
 
+    lax.fori_loop(4, 8, pairs_slope, 0)
     lax.fori_loop(3, 9, nodes_slope, 0)
     node_slope(126)
 
@@ -470,11 +477,16 @@
 
     keep_acc(TIPS + 127, outside * chain_slope)
 
-    def node_down(node, pre):
+    def node_down(base, node, pre):
         keep_acc(TIPS + node, pre * slope[node])
-        above[node] = dot(packed[node], pack_vector(*halves(pre)))
-
-    node_down(126, beside)
+        made = dot(packed[node], pack_vector(*halves(pre)))
+        if base == 0:
+            keep_acc(node, made * tip_slope[node])
+            keep_acc(node + 64, made * tip_slope[node + 64])
+        else:
+            above[node] = made
+
+    node_down(126, 126, beside)
 
     for level in range(6, 0, -1):
         base, after = LEVEL_BASE[level - 1], LEVEL_BASE[level]
@@ -486,21 +498,11 @@
                 m = turn * batch + part
                 left, right = base + m, base + pairs + m
                 over = above[after + m] * norm[after + m][:1]
-                node_down(left, over * message[right])
-                node_down(right, over * message[left])
+                node_down(base, left, over * message[right])
+                node_down(base, right, over * message[left])
             return carry
 
         lax.fori_loop(0, pairs // batch, pairs_down, 0)
-
-    def tips_down(turn, carry):
-        for part in range(2):
-            m = turn * 2 + part
-            over = above[m]
-            keep_acc(m, over * tip_message[m + 64] * tip_slope[m])
-            keep_acc(m + 64, over * tip_message[m] * tip_slope[m + 64])
-        return carry
-
-    lax.fori_loop(0, 32, tips_down, 0)
 
     def total_of(which):
         start = 8 * TIPS * which
@@ -522,9 +524,7 @@
     total = sum_all[0]
     for k in range(1, site_devs):
         total = total + sum_all[k]
-    local_out[:, 0:128] = total[0:1]
-    local_out[:, 128:254] = total[1:2, :126]
-    upper_out[...] = total[1:2, 126:128]
+    out_ref[...] = total[0:2]
     wait_all(chain_all.at[0 : groups - 1], chain_send)
     wait_all(lift_all.at[0 : groups - 1], lift_send)
     wait_all(z_out.at[0 : groups - 1], z_send)
@@ -538,11 +538,11 @@
     smem = pl.BlockSpec(memory_space=pltpu.SMEM)
     V = pltpu.VMEM
     D = pltpu.SemaphoreType.DMA
-    return pl.pallas_call(
+    total = pl.pallas_call(
         kernel,
-        out_shape=(V((1, 254), f32), V((1, 2), f32)),
+        out_shape=V((2, LANES), f32),
         in_specs=[vmem] * 6 + [smem],
-        out_specs=(vmem, vmem),
+        out_specs=vmem,
         scratch_shapes=[
             V((8, LANES), f32), V((8, LANES), i32),
             V((32, LANES), f32),
@@ -580,6 +580,7 @@
         ),
         cost_estimate=pl.CostEstimate(flops=312_000_000, bytes_accessed=200_000, transcendentals=200_000),
     )(tip_states, local_len, upper_len, parent_lists, exchange, freqs.reshape(1, STATES), gamma_rates)
+    return total.reshape(1, 2 * LANES)[:, :254], total[1:, 126:]
 
 
 def solution(mesh):

time: 39.4 us -> 38.1 us (0.967)
  Pallas kernels: 37.5 us -> 36.1 us
    pallas_call x1, Pallas kernels: 37.5 us -> 36.1 us  [per_device(): pl.pallas_call(kernel, out_shape=V((2, LANES), f32), in_specs=[vmem] * 6...]
    slice x0 -> x1, local copies, waits for them, and re-layouts: none -> 0.58 us  [per_device(): return (total.reshape(1, 2 * LANES)[:, :254], total[1:, 126:])]
    unnamed x2 -> x1, local copies, waits for them, and re-layouts: 1.07 us -> 0.56 us
where the time goes in v4:
time: 38.1 us; the launch traced here: 37.9 us
  Pallas kernels  36.1 us (95%)
  local copies, waits for them, and re-layouts  1.14 us (3%)
  between operations  0.64 us (2%)
    pallas_call x1, Pallas kernels, per_device(): pl.pallas_call(kernel, out_shape=V((2, LANES), f32), in_specs=[vmem] * 6...  36.1 us

profile of v4, /device:TPU:0, one launch (start us, length us, event | category | flops | bytes accessed | tf_op | source)
XLA Modules:
  0.0 37.9 jit_solution(1612616820742606927)
XLA Ops:
  0.6 36.1 %shard_map.86 = f32[2,128]{1,0:T(2,128)S(1)} custom-call(s32[128,128]{1,0:T(8,128)} %tips_ref.1, f32[1,254]{1,0:T(1,128)} %local_ref.1, f32[1,2]{1,0:T(1,128)} %upper_ref.1, s32[1,254]{1,0:T(1,128)} %parents_ref.1, f32[20,20]{1,0:T(8,128)} %exchange_ref.1, f32[1,20]{1,0:T(1,128)} %bitcast.4, f32[4]{0:T(128)} %gamma_ref.1), custom_call_target="tpu_custom_call" | custom-call | flops 312000000 | bytes 200000 | tf_op jit(solution)/shard_map/pallas_call | solution.py:541
  36.8 0.6 %slice.7 = f32[1,2]{1,0:T(1,128)} slice(f32[2,128]{1,0:T(2,128)S(1)} %shard_map.86), slice={[1:2], [126:128]} | slice | bytes 16 | tf_op jit(solution)/shard_map/slice | solution.py:583
  37.4 0.6 %copy.10 = f32[1,254]{1,0:T(1,128)} copy(f32[1,254]{1,0:T(1,128)S(1)} %bitcast.3) | data formatting | bytes 2032

commit v5 on v4

--- a/solution.py
+++ b/solution.py
@@ -283,12 +283,12 @@
         for octet in range(2):
 
             def rows(turn, carry):
-                for part in range(4):
-                    r = 4 * turn + part
+                for part in range(8):
+                    r = 8 * turn + part
                     table_row(kind, 8 * octet + r, octet, r)
                 return carry
 
-            lax.fori_loop(0, 2, rows, 0)
+            lax.fori_loop(0, 1, rows, 0)
 
         for r in range(4):
             table_row(kind, 16 + r, 2, r)
@@ -361,7 +361,7 @@
     for level in range(1, 7):
         base, after = LEVEL_BASE[level - 1], LEVEL_BASE[level]
         pairs = 64 >> level
-        batch = min(pairs, 16)
+        batch = min(pairs, 32)
 
         def pairs_up(turn, carry):
             for part in range(batch):

time: 38.1 us -> 37.1 us (0.974)
  Pallas kernels: 36.1 us -> 35 us
    pallas_call x1, Pallas kernels: 36.1 us -> 35 us  [per_device(): pl.pallas_call(kernel, out_shape=V((2, LANES), f32), in_specs=[vmem] * 6...]
where the time goes in v5:
time: 37.1 us; the launch traced here: 36.8 us
  Pallas kernels  35 us (94%)
  local copies, waits for them, and re-layouts  1.14 us (3%)
  between operations  0.64 us (2%)
    pallas_call x1, Pallas kernels, per_device(): pl.pallas_call(kernel, out_shape=V((2, LANES), f32), in_specs=[vmem] * 6...  35 us

profile of v5, /device:TPU:0, one launch (start us, length us, event | category | flops | bytes accessed | tf_op | source)
XLA Modules:
  0.0 36.8 jit_solution(2681090702945805966)
XLA Ops:
  0.6 35.0 %shard_map.86 = f32[2,128]{1,0:T(2,128)S(1)} custom-call(s32[128,128]{1,0:T(8,128)} %tips_ref.1, f32[1,254]{1,0:T(1,128)} %local_ref.1, f32[1,2]{1,0:T(1,128)} %upper_ref.1, s32[1,254]{1,0:T(1,128)} %parents_ref.1, f32[20,20]{1,0:T(8,128)} %exchange_ref.1, f32[1,20]{1,0:T(1,128)} %bitcast.4, f32[4]{0:T(128)} %gamma_ref.1), custom_call_target="tpu_custom_call" | custom-call | flops 312000000 | bytes 200000 | tf_op jit(solution)/shard_map/pallas_call | solution.py:541
  35.7 0.6 %slice.7 = f32[1,2]{1,0:T(1,128)} slice(f32[2,128]{1,0:T(2,128)S(1)} %shard_map.86), slice={[1:2], [126:128]} | slice | bytes 16 | tf_op jit(solution)/shard_map/slice | solution.py:583
  36.3 0.6 %copy.10 = f32[1,254]{1,0:T(1,128)} copy(f32[1,254]{1,0:T(1,128)S(1)} %bitcast.3) | data formatting | bytes 2032
